TPU v7x, 256 devices: a whole 4x4x8 slice. The times are simulated.
256 devices in a mesh: seq: 32 (over y_hi, z, core), mp: 2 (over y_lo), batch: 4 (over x).
Axes of the slice: x: 4, y: 4 (y_hi: 2, y_lo: 2; y = y_hi * 2 + y_lo), z: 8, core: 2. Of those that a mesh axis runs over, the one named last changes fastest.
Arguments:
- conv_input: bfloat16 [4, 65536, 768], P('batch', 'seq'), may hold values from -6 to 6
- pre_activation: bfloat16 [4, 65536, 768], P('batch', 'seq', 'mp'), may hold values from -6 to 6
- track_gradient: bfloat16 [4, 65536, 768], P('batch', 'seq', 'mp'), may hold values from -6 to 6
- kernel: bfloat16 [5, 768, 768], P(None, None, 'mp'), may hold values from -0.09375 to 0.09375
- pair_rows: int32 [4, 16384, 2], P('batch', 'seq'), may hold values from 0 to 65535, as said below
- pair_count: int32 [4, 32], P('batch', 'seq'), may hold values from 256 to 512
- pair_gradient: bfloat16 [4, 16384, 2, 768], P('batch', 'seq', None, 'mp'), may hold values from -6 to 6
Outputs:
- grad_skip: bfloat16 [4, 65536, 768], P('batch', ('seq', 'mp'))
- grad_lower: bfloat16 [4, 32768, 768], P('batch', ('seq', 'mp'))
- grad_weight: float32 [5, 768, 768], P(None, 'seq', 'mp')
Inputs may be any that keep to these rules, and one draw needn't show every extreme that they name: `pair_rows`: A window's pair slots stand in 32 blocks of 512, block s on index s of seq, and the rows of index t of seq are t * 2048 to (t + 1) * 2048 - 1. In every block at most 96 of the 1024 endpoints (padding slots included) lie in the rows of any one index of seq, and in every window one index of seq holds exactly 96 endpoints of every block. A pair's donor row is not above its acceptor row. The first pair_count slots of a block are real pairs; the others are padding whose gradients count for nothing.
All inputs are finite; a program needn't handle non-finite values.
Results may differ from a plain program's by a relative error of at most 0.0049.
Values may be sent and summed in bfloat16 or wider, within the bound.
A program may use at most 128 MiB of HBM per device.

v0:
```python
import jax
import jax.numpy as jnp
from jax import lax
from jax.sharding import PartitionSpec as P

root_half = 0.7071067811865476
inv_root_tau = 0.3989422804014327


def extended(cells, sides, width):
    for axis, dim in sides:
        count = lax.axis_size(axis)
        ends = count - 1
        head = lax.slice_in_dim(cells, 0, width, axis=dim)
        tail = lax.slice_in_dim(cells, cells.shape[dim] - width, cells.shape[dim], axis=dim)
        cells = jnp.concatenate(
            [
                lax.ppermute(tail, axis, [(i, (i + 1) % count) for i in range(ends)]),
                cells,
                lax.ppermute(head, axis, [((i + 1) % count, i) for i in range(ends)]),
            ],
            axis=dim,
        )
    return cells


def gelu_slope(values):
    normal_cdf = 0.5 * (1.0 + lax.erf(values * root_half))
    return normal_cdf + values * inv_root_tau * jnp.exp(-0.5 * values * values)


def conv_rows(padded, kernel_part, begin_row, row_count, reach_rows):
    running = None
    for position in range(kernel_part.shape[0]):
        window_rows = lax.dynamic_slice_in_dim(
            padded, begin_row + 2 * reach_rows - position, row_count, 0
        )
        product = lax.dot_general(
            window_rows,
            kernel_part[position],
            (((1,), (1,)), ((), ())),
            preferred_element_type=jnp.float32,
        )
        running = product if running is None else running + product
    return running


def shards(
    conv_input, pre_activation, track_gradient, kernel, pair_rows, pair_count, pair_gradient
):
    local_rows = track_gradient.shape[1]
    width_local = track_gradient.shape[2]
    tap_count = kernel.shape[0]
    reach_rows = tap_count // 2
    seq_count = lax.axis_size("seq")
    pairs_local = pair_rows.shape[1]
    capacity = min(2 * pairs_local, 6 * pairs_local // seq_count)
    endpoints = 2 * pairs_local
    row_ids = pair_rows[0].reshape(endpoints)
    end_grads = pair_gradient[0].reshape(endpoints, width_local)
    is_valid = jnp.arange(endpoints, dtype=jnp.int32) // 2 < pair_count[0, 0]
    owners = row_ids // local_rows
    offsets = row_ids - owners * local_rows
    owner_hits = (owners[:, None] == jnp.arange(seq_count, dtype=jnp.int32)[None, :]).astype(
        jnp.int32
    )
    ranks = jnp.sum((jnp.cumsum(owner_hits, axis=0) - 1) * owner_hits, axis=1)
    slots = owners * capacity + ranks
    kept_grads = jnp.where(is_valid[:, None], end_grads, jnp.zeros_like(end_grads))
    send_grads = (
        jnp.zeros((seq_count * capacity, width_local), jnp.bfloat16).at[slots].set(kept_grads)
    )
    send_offsets = (
        jnp.full((seq_count * capacity,), local_rows, jnp.int32)
        .at[slots]
        .set(jnp.where(is_valid, offsets, local_rows))
    )
    got_grads, got_offsets = (
        lax.all_to_all(
            send_grads.reshape(seq_count, capacity, width_local),
            "seq",
            split_axis=0,
            concat_axis=0,
            tiled=True,
        ),
        lax.all_to_all(
            send_offsets.reshape(seq_count, capacity),
            "seq",
            split_axis=0,
            concat_axis=0,
            tiled=True,
        ),
    )
    out_grad = (
        track_gradient[0]
        .astype(jnp.float32)
        .at[got_offsets.reshape(seq_count * capacity)]
        .add(got_grads.reshape(seq_count * capacity, width_local).astype(jnp.float32), mode="drop")
    )
    slope_grad = (out_grad * gelu_slope(pre_activation[0].astype(jnp.float32))).astype(jnp.bfloat16)
    padded = extended(slope_grad, (("seq", 0),), 2)
    inputs_local = conv_input[0]
    kernel_pieces = []
    for position in range(tap_count):
        begin_row = 2 * reach_rows - position
        window_rows = padded[begin_row : begin_row + local_rows]
        kernel_pieces.append(
            lax.dot_general(
                inputs_local,
                window_rows,
                (((0,), (0,)), ((), ())),
                preferred_element_type=jnp.float32,
            )
        )
    kernel_local = jnp.stack(kernel_pieces)
    share_rows = local_rows // lax.axis_size("mp")
    input_grad = lax.psum_scatter(
        conv_rows(padded, kernel, jnp.int32(0), lax.axis_size("mp") * share_rows, reach_rows),
        "mp",
        scatter_dimension=0,
        tiled=True,
    )
    channels = input_grad.shape[1]
    grad_skip = input_grad.astype(jnp.bfloat16)[None]
    grad_lower = (
        input_grad.reshape(share_rows // 2, 2, channels).sum(axis=1).astype(jnp.bfloat16)[None]
    )
    total_rows = local_rows * seq_count * lax.axis_size("batch")
    scale_factor = total_rows ** (-0.5)
    summed = lax.psum(kernel_local, ("seq", "batch"))
    piece_rows = summed.shape[1] // seq_count
    kernel_grad = lax.dynamic_slice_in_dim(
        summed, lax.axis_index("seq") * piece_rows, piece_rows, 1
    )
    return (grad_skip, grad_lower, kernel_grad * scale_factor)


def solution(mesh):
    in_specs = (
        P("batch", "seq", None),
        P("batch", "seq", "mp"),
        P("batch", "seq", "mp"),
        P(None, None, "mp"),
        P("batch", "seq", None),
        P("batch", "seq"),
        P("batch", "seq", None, "mp"),
    )
    out_specs = (
        P("batch", ("seq", "mp"), None),
        P("batch", ("seq", "mp"), None),
        P(None, "seq", "mp"),
    )
    return jax.shard_map(shards, mesh=mesh, in_specs=in_specs, out_specs=out_specs, check_vma=False)
```

profile of v0, /device:TPU:1, one launch (start us, length us, event | category | flops | bytes accessed | tf_op | source)
XLA Modules:
  0.0 1458.5 jit_solution(8558860955452167649)
XLA Ops:
  8.0 0.0 copy-start
  8.0 1.0 copy.11
  9.0 0.2 reshape_squeeze.12
  9.2 0.2 reshape_squeeze.11
  9.3 0.2 reshape_squeeze.10
  9.6 9.0 reduce-window.6
  18.6 0.1 slice.44
  18.7 0.1 copy.14
  18.8 0.1 copy.15
  18.9 0.1 add_add_fusion.1
  19.8 4.3 scatter_custom_fusion
  24.1 0.7 all_to_all.9
  24.8 12.8 all-to-all-start
  37.6 3.0 reshape_squeeze.13
  40.5 7.7 scatter_custom_fusion.1
  48.3 0.0 all-to-all-done
  48.3 9.9 all-to-all-start.1
  58.1 0.0 all-reduce.2.cloned.1.call-start
  58.2 3.3 bitcast_convert_fusion
  61.5 0.5 broadcast.223
  62.0 0.7 reduce.3
  62.7 0.1 reshape.198
  62.8 52.1 %all-to-all-done.1 = bf16[32,96,384]{2,1,0:T(8,128)(2,1)} async-done(((bf16[32,96,384]{2,1,0:T(8,128)(2,1)}), bf16[32,96,384]{2,1,0:T(8,128)(2,1)}, u32[]{:S(2)}, u32[]{:S(2)}) %all-to-all-start.1) | async-done | bytes 2359328 | tf_op jit(solution)/shard_map/all_to_all | solution.py:79
  114.9 22.8 %scatter_custom_fusion.2 = f32[2048,384]{1,0:T(8,128)} fusion(f32[2048,384]{1,0:T(8,128)} %bitcast_convert_fusion, s32[3072]{0:T(1024)S(1)} %bitcast.117, bf16[3072,384]{1,0:T(8,128)(2,1)} %bitcast.30), kind=kCustom, calls=%fused_computation.8 | custom fusion | flops 2359296 | bytes 5505024 | tf_op jit(solution)/shard_map/scatter-add | solution.py:98
  137.7 3.1 fusion.19
  140.8 0.0 copy-start.2
  140.8 2.9 collective-permute-start
  143.7 4.6 collective-permute-start.1
  148.3 0.0 collective-permute-done
  148.3 0.0 copy-done
  148.3 2.5 fusion.25
  150.8 2.5 fusion.31
  153.3 2.5 fusion.37
  155.8 0.0 collective-permute-done.1
  155.8 2.5 fusion.43
  158.2 0.0 copy-done.2
  158.2 2.5 fusion.49
  160.7 0.0 copy-start.3
  160.7 0.0 all-reduce.2.cloned.1.call-update
  160.8 0.3 reduce-scatter.2.cloned.1.call-start
  161.0 1.1 copy-done.3
  162.1 0.0 copy-start.4
  162.1 5.7 fusion.61
  167.8 0.0 copy-done.4
  167.8 1.8 fusion.59
  169.7 1.8 fusion.64
  171.5 4.5 fusion.54
  176.0 7.7 add_add_fusion
  183.7 0.0 reduce-scatter.2.cloned.1.call-update
  183.7 1249.4 %all-reduce.2.cloned.1.call-done = f32[5,768,384]{1,2,0:T(8,128)} async-done(((f32[5,768,384]{1,2,0:T(8,128)}), f32[5,768,384]{1,2,0:T(8,128)}) %all-reduce.2.cloned.1.call-update) | async-done | bytes 5898256 | tf_op jit(solution)/shard_map/psum | solution.py:130
  1433.1 1.9 dynamic-slice_multiply_fusion
  1435.0 1.0 copy.16
  1436.0 0.0 reduce-scatter.2.cloned.1.call-done
  1436.0 5.2 reshape.200
  1441.2 0.0 copy-start.1
  1441.2 6.7 reduce_sum.22
  1447.9 3.2 convert_bitcast_fusion
  1451.1 0.0 copy-done.1
  (10 shorter events, 0.2 us)
Async XLA Ops:
  8.0 140.3 %copy-start = (bf16[1,2048,768]{2,1,0:T(8,128)(2,1)S(1)}, bf16[1,2048,768]{2,1,0:T(8,128)(2,1)}, u32[]{:S(2)}) copy-start(bf16[1,2048,768]{2,1,0:T(8,128)(2,1)} %param.7) | copy-start | bytes 9437188
  24.8 23.5 %all-to-all-start = ((s32[32,1,96]{2,1,0:T(1,128)}), s32[32,1,96]{2,1,0:T(1,128)S(1)}, u32[]{:S(2)}, u32[]{:S(2)}) async-start(s32[32,1,96]{2,1,0:T(1,128)} %all_to_all.9), calls=%async_computation | async-start | bytes 32768 | tf_op jit(solution)/shard_map/all_to_all | solution.py:86
  48.3 66.6 %all-to-all-start.1 = ((bf16[32,96,384]{2,1,0:T(8,128)(2,1)}), bf16[32,96,384]{2,1,0:T(8,128)(2,1)}, u32[]{:S(2)}, u32[]{:S(2)}) async-start(bf16[32,96,384]{2,1,0:T(8,128)(2,1)} %bitcast.112), calls=%async_computation.1 | async-start | bytes 4718592 | tf_op jit(solution)/shard_map/all_to_all | solution.py:79
  58.1 1375.0 %all-reduce.2.cloned.1.call-start = ((), (), s32[]{:S(2)}) async-start(), calls=%async_computation.4 | async-start | bytes 11796480 | tf_op jit(solution)/shard_map/psum | solution.py:130
  140.8 17.5 %copy-start.2 = (bf16[2048,384]{1,0:T(8,128)(2,1)}, bf16[2048,384]{1,0:T(8,128)(2,1)S(1)}, u32[]{:S(2)}) copy-start(bf16[2048,384]{1,0:T(8,128)(2,1)S(1)} %fusion.19) | copy-start | bytes 4718596
  140.8 7.5 collective-permute-start
  143.7 12.0 collective-permute-start.1
  160.7 1.4 copy-start.3
  160.8 1275.2 %reduce-scatter.2.cloned.1.call-start = ((), (), s32[]{:S(2)}) async-start(), calls=%async_computation.3 | async-start | bytes 9437184 | tf_op jit(solution)/shard_map/reduce_scatter | solution.py:117
  162.1 5.7 copy-start.4
  1441.2 9.9 copy-start.1
Sparse Core Ops, SparseCore 0:
  160.9 1272.2 all-reduce.1
Sparse Core Ops, SparseCore 1:
  183.8 80.0 reduce-scatter.1
where the time goes:
time: 1460 us
  waiting for transfers between devices  1300 us (89%)
  other arithmetic  58.6 us (4%)
  matrix products  33.9 us (2%)
  starting transfers between devices  30.4 us (2%)
  local copies, waits for them, and re-layouts  17.7 us (1%)
  between operations  16.3 us (1%)
    psum x1, waiting for transfers between devices, shards(): summed = lax.psum(kernel_local, ('seq', 'batch'))  1250 us
    all_to_all x1, waiting for transfers between devices, shards(): lax.all_to_all(send_grads.reshape(seq_count, capacity, width_local), 'seq...  52.1 us
  transfers between devices with their start and end apart: 6, of which 2 were waited for; matrix products, arithmetic and copies ran while one was open for 3% of the time, Pallas kernels for 0%

commit v1 on v0

--- a/solution.py
+++ b/solution.py
@@ -127,11 +127,14 @@
     )
     total_rows = local_rows * seq_count * lax.axis_size("batch")
     scale_factor = total_rows ** (-0.5)
-    summed = lax.psum(kernel_local, ("seq", "batch"))
-    piece_rows = summed.shape[1] // seq_count
-    kernel_grad = lax.dynamic_slice_in_dim(
-        summed, lax.axis_index("seq") * piece_rows, piece_rows, 1
+    channels_in = kernel_local.shape[1]
+    piece_rows = channels_in // seq_count
+    parts = kernel_local.astype(jnp.bfloat16).reshape(
+        tap_count, seq_count, piece_rows, width_local
     )
+    parts = lax.all_to_all(parts, "seq", split_axis=1, concat_axis=1, tiled=True)
+    piece = jnp.sum(parts.astype(jnp.float32), axis=1)
+    kernel_grad = lax.psum(piece, "batch")
     return (grad_skip, grad_lower, kernel_grad * scale_factor)
 
 

time: 1460 us -> 379 us (0.26)
  waiting for transfers between devices: 1300 us -> 180 us
  local copies, waits for them, and re-layouts: 17.7 us -> 35.8 us
    psum x1, waiting for transfers between devices: 1250 us -> 29.5 us  [shards(): kernel_grad = lax.psum(piece, 'batch')]
    all_to_all x0 -> x1, waiting for transfers between devices: none -> 50.1 us  [shards(): lax.all_to_all(parts, 'seq', split_axis=1, concat_axis=1, tiled=True)]
    reduce_scatter x1, waiting for transfers between devices: 0.01 us -> 48.5 us  [shards(): lax.psum_scatter(conv_rows(padded, kernel, jnp.int32(0), lax.axis_size('m...]
  transfers between devices with their start and end apart: 6 -> 7, of which waited for: 2 -> 4; matrix products, arithmetic and copies ran while one was open for 3% -> 17% of each run, Pallas kernels for 0% -> 0%
where the time goes in v1:
time: 379 us; the launch traced here: 378 us
  waiting for transfers between devices  180 us (47%)
  other arithmetic  61.3 us (16%)
  matrix products  48.3 us (13%)
  local copies, waits for them, and re-layouts  35.8 us (9%)
  starting transfers between devices  35.7 us (9%)
  between operations  16.4 us (4%)
    all_to_all x1, waiting for transfers between devices, shards(): lax.all_to_all(send_grads.reshape(seq_count, capacity, width_local), 'seq...  52.2 us
    all_to_all x1, waiting for transfers between devices, shards(): lax.all_to_all(parts, 'seq', split_axis=1, concat_axis=1, tiled=True)  50.1 us
    reduce_scatter x1, waiting for transfers between devices, shards(): lax.psum_scatter(conv_rows(padded, kernel, jnp.int32(0), lax.axis_size('m...  48.5 us
    dot_general x5, matrix products, conv_rows(): lax.dot_general(window_rows, kernel_part[position], (((1,), (1,)), ((), (...  31.4 us
    psum x1, waiting for transfers between devices, shards(): kernel_grad = lax.psum(piece, 'batch')  29.5 us
    scatter-add x1, other arithmetic, shards(): out_grad = track_gradient[0].astype(jnp.float32).at[got_offsets.reshape(s...  22.8 us
    dot_general x5, matrix products, shards(): lax.dot_general(inputs_local, window_rows, (((0,), (0,)), ((), ())), pref...  16.9 us
    all_to_all x1, starting transfers between devices, shards(): lax.all_to_all(send_offsets.reshape(seq_count, capacity), 'seq', split_ax...  12.8 us
  transfers between devices with their start and end apart: 7, of which 4 were waited for; matrix products, arithmetic and copies ran while one was open for 17% of the time, Pallas kernels for 0%

profile of v1, /device:TPU:1, one launch (start us, length us, event | category | flops | bytes accessed | tf_op | source)
XLA Modules:
  0.0 377.8 jit_solution(16501517123568387448)
XLA Ops:
  8.0 0.0 copy-start
  8.0 1.0 copy.20
  9.0 0.2 reshape_squeeze.12
  9.2 0.2 reshape_squeeze.11
  9.3 0.2 reshape_squeeze.10
  9.6 9.0 %reduce-window.6 = s32[32,8,128]{2,1,0:T(8,128)S(1)} reduce-window(s32[32,8,128]{2,1,0:T(8,128)S(1)} %fusion.74, s32[]{:T(128)} %constant.48.clone.1), window={size=1x1x128 pad=0_0x0_0x127_0}, to_apply=%region_0.1 | reduce-window | flops 4161536 | bytes 262148 | tf_op jit(solution)/shard_map/reduce-window
  18.6 0.1 slice.44
  18.7 0.1 copy.23
  18.8 0.1 copy.24
  18.9 0.1 add_add_fusion.1
  19.8 4.3 %scatter_custom_fusion = s32[3072]{0:T(1024)S(1)} fusion(s32[1024]{0:T(1024)S(1)} %bitcast.108, s32[1024]{0:T(1024)S(1)} %get-tuple-element.5, s32[]{:T(128)} %constant.46.clone.1), kind=kCustom, calls=%fused_computation.101 | custom fusion | bytes 12292 | tf_op jit(solution)/shard_map/scatter | solution.py:76
  24.1 0.7 all_to_all.12
  24.8 12.8 %all-to-all-start = ((s32[32,1,96]{2,1,0:T(1,128)}), s32[32,1,96]{2,1,0:T(1,128)S(1)}, u32[]{:S(2)}, u32[]{:S(2)}) async-start(s32[32,1,96]{2,1,0:T(1,128)} %all_to_all.12), calls=%async_computation | async-start | bytes 32768 | tf_op jit(solution)/shard_map/all_to_all | solution.py:86
  37.6 3.0 reshape_squeeze.13
  40.5 7.7 %scatter_custom_fusion.1 = bf16[3072,384]{1,0:T(8,128)(2,1)} fusion(s32[1024]{0:T(1024)S(1)} %bitcast.109, bf16[]{:T(256)} %constant.54.clone.1, bf16[1024,384]{1,0:T(8,128)(2,1)} %reshape_squeeze.13, pred[1024]{0:T(1024)(128)(4,1)S(1)} %fusion.79), kind=kCustom, calls=%fused_computation.49 | custom fusion | flops 393216 | bytes 3147776 | tf_op jit(solution)/shard_map/scatter | solution.py:71
  48.3 0.0 all-to-all-done
  48.3 9.9 %all-to-all-start.1 = ((bf16[32,96,384]{2,1,0:T(8,128)(2,1)}), bf16[32,96,384]{2,1,0:T(8,128)(2,1)}, u32[]{:S(2)}, u32[]{:S(2)}) async-start(bf16[32,96,384]{2,1,0:T(8,128)(2,1)} %bitcast.97), calls=%async_computation.1 | async-start | bytes 4718592 | tf_op jit(solution)/shard_map/all_to_all | solution.py:79
  58.1 3.3 bitcast_convert_fusion
  61.4 0.5 broadcast.223
  61.9 0.7 reduce.3
  62.6 0.1 reshape.214
  62.7 52.2 %all-to-all-done.1 = bf16[32,96,384]{2,1,0:T(8,128)(2,1)} async-done(((bf16[32,96,384]{2,1,0:T(8,128)(2,1)}), bf16[32,96,384]{2,1,0:T(8,128)(2,1)}, u32[]{:S(2)}, u32[]{:S(2)}) %all-to-all-start.1) | async-done | bytes 2359328 | tf_op jit(solution)/shard_map/all_to_all | solution.py:79
  114.9 22.8 %scatter_custom_fusion.2 = f32[2048,384]{1,0:T(8,128)} fusion(f32[2048,384]{1,0:T(8,128)} %bitcast_convert_fusion, s32[3072]{0:T(1024)S(1)} %bitcast.107, bf16[3072,384]{1,0:T(8,128)(2,1)} %bitcast.30), kind=kCustom, calls=%fused_computation.9 | custom fusion | flops 2359296 | bytes 5505024 | tf_op jit(solution)/shard_map/scatter-add | solution.py:98
  137.7 3.1 fusion.19
  140.8 0.0 copy-start.2
  140.8 5.4 %collective-permute-start.1 = (bf16[2,384]{1,0:T(2,128)(2,1)S(1)}, bf16[2,384]{1,0:T(2,128)(2,1)S(1)}, u32[]{:S(2)}, u32[]{:S(2)}) collective-permute-start(bf16[2,384]{1,0:T(2,128)(2,1)S(1)} %get-tuple-element.4), channel_id=1, source_target_pairs={{0,8},{8,16},{16,24},{24,32},{32,40},{40,48},{48,56},{56,64},{64,7... | collective-permute-start | bytes 4616 | tf_op jit(solution)/shard_map/ppermute | solution.py:18
  146.2 2.1 collective-permute-start
  148.3 2.3 fusion.43
  150.6 2.1 copy.27
  152.7 0.0 collective-permute-done
  152.7 3.7 fusion.49
  156.4 2.1 copy.25
  158.5 3.7 fusion.46
  162.2 0.9 constant_dynamic-update-slice_fusion.4
  163.1 2.1 copy.26
  165.2 0.0 collective-permute-done.1
  165.2 3.7 fusion.40
  168.8 2.1 copy.28
  171.0 3.6 fusion.37
  174.6 1.4 copy.29
  176.0 1.9 constant_dynamic-update-slice_fusion.3
  178.0 2.0 constant_dynamic-update-slice_fusion.2
  180.0 0.9 constant_dynamic-update-slice_fusion.1
  180.8 0.9 constant_dynamic-update-slice_fusion
  181.7 3.8 %copy.30 = bf16[5,32,24,384]{3,2,0,1:T(8,128)(2,1)} copy(bf16[5,32,24,384]{3,2,1,0:T(8,128)(2,1)} %constant_dynamic-update-slice_fusion) | data formatting | bytes 5898240 | tf_op jit(solution)/shard_map/stack | solution.py:115
  185.5 5.0 %all-to-all-start.2 = ((bf16[5,32,24,384]{3,2,0,1:T(8,128)(2,1)}), bf16[5,32,24,384]{3,2,0,1:T(8,128)(2,1)}, u32[]{:S(2)}, u32[]{:S(2)}) async-start(bf16[5,32,24,384]{3,2,0,1:T(8,128)(2,1)} %copy.30), calls=%async_computation.3 | async-start | bytes 5898240 | tf_op jit(solution)/shard_map/all_to_all | solution.py:135
  190.6 0.3 all-reduce.2.cloned.1.call-start
  190.8 0.0 copy-start.4
  190.8 5.7 %fusion.61 = f32[2048,768]{1,0:T(8,128)} fusion(bf16[2048,384]{1,0:T(8,128)(2,1)S(1)} %copy-done.3, bf16[5,768,384]{2,1,0:T(8,128)(2,1)} %param.10), kind=kOutput, calls=%fused_computation.59 | convolution fusion | flops 1207959552 | bytes 8454144 | tf_op jit(solution)/shard_map/dot_general | solution.py:38
  196.6 4.4 %fusion.59 = f32[2048,768]{1,0:T(8,128)} fusion(bf16[5,768,384]{2,1,0:T(8,128)(2,1)S(1)} %copy-done.4, bf16[2,384]{1,0:T(2,128)(2,1)S(1)} %collective-permute-done.1, bf16[2048,384]{1,0:T(8,128)(2,1)S(1)} %copy-done.3), kind=kOutput, calls=%fused_computation.57 | convolution fusion | flops 1211105280 | bytes 8455680 | tf_op jit(solution)/shard_map/dot_general | solution.py:38
  201.0 4.5 %fusion.64 = f32[2048,768]{1,0:T(8,128)} fusion(bf16[5,768,384]{2,1,0:T(8,128)(2,1)S(1)} %copy-done.4, bf16[2048,384]{1,0:T(8,128)(2,1)S(1)} %copy-done.3, bf16[2,384]{1,0:T(2,128)(2,1)S(1)} %collective-permute-done), kind=kOutput, calls=%fused_computation.62 | convolution fusion | flops 1211105280 | bytes 8455680 | tf_op jit(solution)/shard_map/dot_general | solution.py:38
  205.5 4.4 %fusion.54 = f32[2048,768]{1,0:T(8,128)} fusion(bf16[2,384]{1,0:T(2,128)(2,1)S(1)} %collective-permute-done, bf16[2048,384]{1,0:T(8,128)(2,1)S(1)} %copy-done.3, bf16[5,768,384]{2,1,0:T(8,128)(2,1)S(1)} %copy-done.4), kind=kOutput, calls=%fused_computation.51 | convolution fusion | flops 1211105280 | bytes 8455680 | tf_op jit(solution)/shard_map/dot_general | solution.py:38
  209.9 50.1 %all-to-all-done.2 = bf16[5,32,24,384]{3,2,0,1:T(8,128)(2,1)} async-done(((bf16[5,32,24,384]{3,2,0,1:T(8,128)(2,1)}), bf16[5,32,24,384]{3,2,0,1:T(8,128)(2,1)}, u32[]{:S(2)}, u32[]{:S(2)}) %all-to-all-start.2) | async-done | bytes 2949152 | tf_op jit(solution)/shard_map/all_to_all | solution.py:135
  260.0 2.9 convert_reduce_fusion
  262.9 0.0 all-reduce.2.cloned.1.call-update
  262.9 0.3 reduce-scatter.2.cloned.1.call-start
  263.3 12.3 %add_add_fusion = f32[2048,768]{1,0:T(8,128)} fusion(f32[2048,768]{1,0:T(8,128)} %fusion.59, f32[2048,768]{1,0:T(8,128)} %fusion.61, f32[2048,768]{1,0:T(8,128)} %fusion.64, f32[2048,768]{1,0:T(8,128)} %fusion.54, bf16[2048,384]{1,0:T(8,128)(2,1)S(1)} %copy-done.3, bf16[2,384]{1,0:T(2,128)(2,1)S(1)} %collective-permute-done.1, bf16[5,768,384]{2,1,0:T(8,128)(2,1)} %param.10), kind=kOutput, calls=%fused_computation.3 | convolution fusion | flops 1217396736 | bytes 33621504 | tf_op jit(solution)/shard_map/dot_general | solution.py:38
  275.6 0.0 reduce-scatter.2.cloned.1.call-update
  275.6 29.5 %all-reduce.2.cloned.1.call-done = f32[5,24,384]{2,1,0:T(8,128)} async-done(((f32[5,24,384]{2,1,0:T(8,128)}), f32[5,24,384]{2,1,0:T(8,128)}) %all-reduce.2.cloned.1.call-update) | async-done | bytes 184336 | tf_op jit(solution)/shard_map/psum | solution.py:137
  305.1 1.6 broadcast_multiply_fusion
  306.7 48.5 %reduce-scatter.2.cloned.1.call-done = f32[1024,768]{1,0:T(8,128)} async-done(((f32[2048,768]{1,0:T(8,128)}), f32[1024,768]{1,0:T(8,128)}) %reduce-scatter.2.cloned.1.call-update) | async-done | bytes 3145744 | tf_op jit(solution)/shard_map/reduce_scatter | solution.py:117
  355.3 5.2 %reshape.216 = f32[512,2,768]{2,1,0:T(2,128)} reshape(f32[1024,768]{1,0:T(8,128)} %reduce-scatter.2.cloned.1.call-done) | data formatting | bytes 6291456 | tf_op jit(solution)/shard_map/reshape | solution.py:126
  360.4 6.7 %reduce_sum.31 = bf16[512,768]{1,0:T(8,128)(2,1)} reduce(f32[512,2,768]{2,1,0:T(2,128)} %reshape.216, f32[]{:T(128)} %constant.60.clone.1), dimensions={1}, to_apply=%region_7.8 | reduce | flops 393216 | bytes 3932164 | tf_op jit(solution)/shard_map/reduce_sum | solution.py:126
  367.2 3.2 convert_bitcast_fusion
  (21 shorter events, 0.2 us)
Async XLA Ops:
  8.0 140.3 %copy-start = (bf16[1,2048,768]{2,1,0:T(8,128)(2,1)S(1)}, bf16[1,2048,768]{2,1,0:T(8,128)(2,1)}, u32[]{:S(2)}) copy-start(bf16[1,2048,768]{2,1,0:T(8,128)(2,1)} %param.7) | copy-start | bytes 9437188
  24.8 23.5 %all-to-all-start = ((s32[32,1,96]{2,1,0:T(1,128)}), s32[32,1,96]{2,1,0:T(1,128)S(1)}, u32[]{:S(2)}, u32[]{:S(2)}) async-start(s32[32,1,96]{2,1,0:T(1,128)} %all_to_all.12), calls=%async_computation | async-start | bytes 32768 | tf_op jit(solution)/shard_map/all_to_all | solution.py:86
  48.3 66.6 %all-to-all-start.1 = ((bf16[32,96,384]{2,1,0:T(8,128)(2,1)}), bf16[32,96,384]{2,1,0:T(8,128)(2,1)}, u32[]{:S(2)}, u32[]{:S(2)}) async-start(bf16[32,96,384]{2,1,0:T(8,128)(2,1)} %bitcast.97), calls=%async_computation.1 | async-start | bytes 4718592 | tf_op jit(solution)/shard_map/all_to_all | solution.py:79
  140.8 7.6 %copy-start.2 = (bf16[2048,384]{1,0:T(8,128)(2,1)}, bf16[2048,384]{1,0:T(8,128)(2,1)S(1)}, u32[]{:S(2)}) copy-start(bf16[2048,384]{1,0:T(8,128)(2,1)S(1)} %fusion.19) | copy-start | bytes 4718596
  140.8 24.4 %collective-permute-start.1 = (bf16[2,384]{1,0:T(2,128)(2,1)S(1)}, bf16[2,384]{1,0:T(2,128)(2,1)S(1)}, u32[]{:S(2)}, u32[]{:S(2)}) collective-permute-start(bf16[2,384]{1,0:T(2,128)(2,1)S(1)} %get-tuple-element.4), channel_id=1, source_target_pairs={{0,8},{8,16},{16,24},{24,32},{32,40},{40,48},{48,56},{56,64},{64,7... | collective-permute-start | bytes 4616 | tf_op jit(solution)/shard_map/ppermute | solution.py:18
  146.2 6.5 %collective-permute-start = (bf16[2,384]{1,0:T(2,128)(2,1)S(1)}, bf16[2,384]{1,0:T(2,128)(2,1)S(1)}, u32[]{:S(2)}, u32[]{:S(2)}) collective-permute-start(bf16[2,384]{1,0:T(2,128)(2,1)S(1)} %get-tuple-element.3), channel_id=1, source_target_pairs={{8,0},{16,8},{24,16},{32,24},{40,32},{48,40},{56,48},{64,56},{72,6... | collective-permute-start | bytes 4616 | tf_op jit(solution)/shard_map/ppermute | solution.py:20
  158.5 3.7 copy-start.6
  174.6 5.3 %copy-start.5 = (bf16[768,384]{1,0:T(8,128)(2,1)S(1)}, bf16[768,384]{1,0:T(8,128)(2,1)}, u32[]{:S(2)}) copy-start(bf16[768,384]{1,0:T(8,128)(2,1)} %copy.28) | copy-start | bytes 1769476
  185.5 5.3 %copy-start.3 = (bf16[2048,384]{1,0:T(8,128)(2,1)S(1)}, bf16[2048,384]{1,0:T(8,128)(2,1)}, u32[]{:S(2)}) copy-start(bf16[2048,384]{1,0:T(8,128)(2,1)} %copy-done.2) | copy-start | bytes 4718596
  185.5 74.4 %all-to-all-start.2 = ((bf16[5,32,24,384]{3,2,0,1:T(8,128)(2,1)}), bf16[5,32,24,384]{3,2,0,1:T(8,128)(2,1)}, u32[]{:S(2)}, u32[]{:S(2)}) async-start(bf16[5,32,24,384]{3,2,0,1:T(8,128)(2,1)} %copy.30), calls=%async_computation.3 | async-start | bytes 5898240 | tf_op jit(solution)/shard_map/all_to_all | solution.py:135
  190.6 114.6 %all-reduce.2.cloned.1.call-start = ((), (), s32[]{:S(2)}) async-start(), calls=%async_computation.5 | async-start | bytes 368640 | tf_op jit(solution)/shard_map/psum | solution.py:137
  190.8 5.7 %copy-start.4 = (bf16[5,768,384]{2,1,0:T(8,128)(2,1)S(1)}, bf16[5,768,384]{2,1,0:T(8,128)(2,1)}, u32[]{:S(2)}) copy-start(bf16[5,768,384]{2,1,0:T(8,128)(2,1)} %param.10) | copy-start | bytes 8847364
  262.9 92.3 %reduce-scatter.2.cloned.1.call-start = ((), (), s32[]{:S(2)}) async-start(), calls=%async_computation.4 | async-start | bytes 9437184 | tf_op jit(solution)/shard_map/reduce_scatter | solution.py:117
  360.4 9.9 %copy-start.1 = (bf16[1,2048,768]{2,1,0:T(8,128)(2,1)S(1)}, bf16[1,2048,768]{2,1,0:T(8,128)(2,1)}, u32[]{:S(2)}) copy-start(bf16[1,2048,768]{2,1,0:T(8,128)(2,1)} %param.7) | copy-start | bytes 9437188
Sparse Core Ops, SparseCore 0:
  263.1 41.9 all-reduce.1
Sparse Core Ops, SparseCore 1:
  275.7 79.5 reduce-scatter.1

commit v2 on v0

v2 whole, which is shorter than its diff:
```python
import functools

import jax
import jax.numpy as jnp
from jax import lax
from jax.experimental import pallas as pl
from jax.experimental.pallas import tpu as pltpu
from jax.sharding import PartitionSpec as P

MESH = pl.DeviceIdType.MESH
F32 = jnp.float32
BF16 = jnp.bfloat16
root_half = 0.7071067811865476
inv_root_tau = 0.3989422804014327
TILE = 256
BORDER = 16
CHUNKS = 4
PACK = 4
SLOT_ROWS = 128


def gelu_slope(values):
    normal_cdf = 0.5 * (1.0 + lax.erf(values * root_half))
    return normal_cdf + values * inv_root_tau * jnp.exp(-0.5 * values * values)


def body(
    sizes,
    rows_ref, count_ref, pairs_ref, track_ref, pre_ref, conv_ref, kern_ref,
    skip_ref, lower_ref, weight_ref,
    pairs_v, slot_v, onehot_v, send_v, recv_v, soff_v, roff_v,
    track_v, pre_v, conv_v, convt_v, slope_f, grad_v, kfull_v,
    share_v, other_v, other_f, wins_v, acc_v,
    wb_v, wa_v, wsb_v, wrb_v, wown_v, wsc_v, wrc_v, wfin_v,
    skip_v, lower_v,
    load_sem, g_send, g_recv, o_send, o_recv, kx_send, kx_recv, kc_send, kc_recv,
    h_send, h_recv, m_send, m_recv, a_send, a_recv, b_send, b_recv,
    c_send, c_recv, d_send, d_recv, out_sem,
):
    n_seq, n_x, cap, rows_dev, width, depth, taps, scale = sizes
    n_chip = n_seq // 2
    n_z = n_chip // 2
    reach = taps // 2
    endpoints = pairs_ref.shape[0]
    share = rows_dev // 2
    tiles = rows_dev // TILE
    share_tiles = share // TILE
    chip_rows = depth // n_chip
    block = wb_v.shape[1]
    half = block // 2
    piece = half // n_x
    per_chunk = n_chip // CHUNKS
    chunk_rows = chip_rows * per_chunk
    quarter = depth // 4

    me = lax.axis_index("seq")
    mp = lax.axis_index("mp")
    xme = lax.axis_index("batch")
    core = lax.rem(me, 2)
    chip = me // 2
    yhi = chip // n_z
    zme = lax.rem(chip, n_z)
    twin = me + 1 - 2 * core

    def at_seq(target):
        return {"seq": target}

    up = {"seq": (lax.rem(yhi + mp, 2) * n_z + zme) * 2 + core, "mp": 1 - mp}
    down = {"seq": (lax.rem(yhi + 1 - mp, 2) * n_z + zme) * 2 + core, "mp": 1 - mp}

    loads = [
        pltpu.make_async_copy(pairs_ref, pairs_v, load_sem.at[0]),
        pltpu.make_async_copy(pre_ref, pre_v, load_sem.at[1]),
        pltpu.make_async_copy(track_ref, track_v, load_sem.at[2]),
        pltpu.make_async_copy(conv_ref, conv_v, load_sem.at[3]),
        pltpu.make_async_copy(kern_ref, kfull_v.at[:, :, pl.ds(0, width)], load_sem.at[4]),
    ]
    for load in loads:
        load.start()

    barrier = pltpu.get_barrier_semaphore()

    def greet(target):
        pl.semaphore_signal(barrier, inc=1, device_id=target, device_id_type=MESH)

    @pl.loop(1, n_seq)
    def _(step):
        greet(at_seq(lax.rem(me + step, n_seq)))

    @pl.loop(1, n_x)
    def _(step):
        peer = lax.rem(xme + step, n_x)
        greet({"batch": peer})
        greet({"seq": twin, "batch": peer})

    greet(up)
    greet(down)

    lane = lax.broadcasted_iota(jnp.int32, (1, endpoints), 1)
    rows = rows_ref[...]
    owner = rows // rows_dev
    offset = rows - owner * rows_dev
    owner = jnp.where(lane // 2 < count_ref[0, 0], owner, n_seq)
    hit = owner == lax.broadcasted_iota(jnp.int32, (n_seq, endpoints), 0)
    rank = hit.astype(jnp.int32)
    wide_lane = lax.broadcasted_iota(jnp.int32, (n_seq, endpoints), 1)
    shift = 1
    while shift < endpoints:
        rank = rank + jnp.where(wide_lane >= shift, pltpu.roll(rank, shift, 1), 0)
        shift *= 2
    slot_v[...] = jnp.where(hit, rank - 1, -1)
    kind = lax.broadcasted_iota(jnp.int32, (16, endpoints), 0)
    parts = jnp.where(kind == 0, offset // 64, jnp.where(kind == 1, lax.rem(offset, 64), 1))
    parts = parts.astype(F32).astype(BF16)

    loads[0].wait()
    pl.semaphore_wait(barrier, (n_seq - 1) + 2 * (n_x - 1) + 2)

    def grads_to(step):
        return pltpu.make_async_remote_copy(
            src_ref=send_v.at[step],
            dst_ref=recv_v.at[pl.ds(pl.multiple_of(step * cap, 16), cap)],
            send_sem=g_send.at[step],
            recv_sem=g_recv.at[step],
            device_id=at_seq(lax.rem(me + step, n_seq)),
            device_id_type=MESH,
        )

    def offsets_to(step):
        return pltpu.make_async_remote_copy(
            src_ref=soff_v.at[step],
            dst_ref=roff_v.at[step],
            send_sem=o_send.at[step],
            recv_sem=o_recv.at[step],
            device_id=at_seq(lax.rem(me + step, n_seq)),
            device_id_type=MESH,
        )

    def pack(first):
        for i in range(PACK):
            target = lax.rem(me + first + i, n_seq)
            slots = slot_v[pl.ds(target, 1), :]
            places = lax.broadcasted_iota(jnp.int32, (SLOT_ROWS, endpoints), 0)
            onehot_v[pl.ds(i * SLOT_ROWS, SLOT_ROWS), :] = jnp.where(
                slots == places, 1.0, 0.0
            ).astype(BF16)
        onehot = onehot_v[...]
        listed = jnp.dot(onehot, pairs_v[...], preferred_element_type=F32).astype(BF16)
        marks = lax.dot_general(
            parts, onehot, (((1,), (1,)), ((), ())), preferred_element_type=F32
        )
        where_to = jnp.where(marks[2:3] > 0.5, marks[0:1] * 64.0 + marks[1:2], -1.0)
        return listed, where_to

    def emit(first, begin):
        listed, where_to = pack(first)
        for i in range(PACK):
            some = listed[i * SLOT_ROWS : i * SLOT_ROWS + cap]
            place = jnp.broadcast_to(
                where_to[:, i * SLOT_ROWS : (i + 1) * SLOT_ROWS], (8, SLOT_ROWS)
            )
            if i < begin:
                recv_v[pl.ds(0, cap), :] = some
                roff_v[0] = place
            else:
                send_v[first + i] = some
                soff_v[first + i] = place
                offsets_to(first + i).start()
                grads_to(first + i).start()

    emit(0, 1)

    @pl.loop(1, n_seq // PACK)
    def _(turn):
        emit(turn * PACK, 0)

    def kernel_piece(index):
        return pl.ds(pl.multiple_of(index * quarter, 16), quarter)

    def kernel_across(way, target):
        return pltpu.make_async_remote_copy(
            src_ref=kern_ref.at[:, kernel_piece(2 * core + way), :],
            dst_ref=kfull_v.at[:, kernel_piece(2 * core + way), pl.ds(width, width)],
            send_sem=kx_send.at[way],
            recv_sem=kx_recv.at[way],
            device_id=target,
            device_id_type=MESH,
        )

    def kernel_twin(way, at_core):
        region = kfull_v.at[:, kernel_piece(2 * at_core + way), pl.ds(width, width)]
        return pltpu.make_async_remote_copy(
            src_ref=region,
            dst_ref=region,
            send_sem=kc_send.at[way],
            recv_sem=kc_recv.at[way],
            device_id=at_seq(twin),
            device_id_type=MESH,
        )

    kernel_across(0, up).start()
    kernel_across(1, down).start()

    loads[1].wait()
    loads[2].wait()

    @pl.loop(0, tiles)
    def _(tile):
        at = pl.ds(pl.multiple_of(tile * TILE, TILE), TILE)
        grad_v[at, :] = gelu_slope(pre_v[at, :].astype(F32))
        slope_f[pl.ds(pl.multiple_of(BORDER + tile * TILE, BORDER), TILE), :] = track_v[
            at, :
        ].astype(F32)

    loads[3].wait()

    @pl.loop(0, tiles)
    def _(tile):
        at = pl.ds(pl.multiple_of(tile * TILE, TILE), TILE)
        turned = conv_v[at, :].T
        for place in range(n_chip):
            source = place // per_chunk + CHUNKS * (place % per_chunk)
            convt_v[pl.ds(place * chip_rows, chip_rows), at] = turned[
                source * chip_rows : (source + 1) * chip_rows
            ]

    for way in range(2):
        kernel_across(way, up).wait_recv()
        kernel_twin(way, core).start()

    tile_lane = lax.broadcasted_iota(jnp.int32, (8, SLOT_ROWS), 1)

    def four_lists(first):
        p = [roff_v[first + i] for i in range(4)]
        one = pltpu.roll(p[1], 96, 1)
        two = pltpu.roll(p[2], 64, 1)
        three = pltpu.roll(p[3], 32, 1)
        return jnp.concatenate(
            [
                jnp.where(tile_lane < 96, p[0], one),
                jnp.where(tile_lane < 64, one, two),
                jnp.where(tile_lane < 32, two, three),
            ],
            axis=1,
        )[0:1]

    groups = [(first, 8) for first in range(0, n_seq - 8, 8)] + [(n_seq - 8, 4), (n_seq - 4, 4)]
    for first, many in groups:

        @pl.loop(max(first, 1), first + many)
        def _(step):
            offsets_to(step).wait_recv()
            grads_to(step).wait_recv()

        lists = jnp.concatenate([four_lists(first + i) for i in range(0, many, 4)], axis=1)

        @pl.loop(0, tiles)
        def _(tile, first=first, many=many, lists=lists):
            row = lax.broadcasted_iota(jnp.int32, (TILE, many * cap), 0) + tile * TILE
            onehot = jnp.where(row.astype(F32) == lists, 1.0, 0.0).astype(BF16)
            at = pl.ds(pl.multiple_of(BORDER + tile * TILE, BORDER), TILE)
            slope_f[at, :] += jnp.dot(
                onehot,
                recv_v[pl.ds(first * cap, many * cap), :],
                preferred_element_type=F32,
            )

    @pl.loop(0, tiles)
    def _(tile):
        at = pl.ds(pl.multiple_of(BORDER + tile * TILE, BORDER), TILE)
        from_at = pl.ds(pl.multiple_of(tile * TILE, TILE), TILE)
        slope_f[at, :] = (slope_f[at, :] * grad_v[from_at, :]).astype(BF16).astype(F32)

    low = pl.ds(BORDER - 8, 8)
    high = pl.ds(BORDER + rows_dev, 8)

    def halo(way, target):
        own = pl.ds(BORDER, 8) if way == 0 else pl.ds(BORDER + rows_dev - 8, 8)
        return pltpu.make_async_remote_copy(
            src_ref=slope_f.at[own],
            dst_ref=slope_f.at[high if way == 0 else low],
            send_sem=h_send.at[way],
            recv_sem=h_recv.at[way],
            device_id=at_seq(target),
            device_id_type=MESH,
        )

    before = lax.rem(me + n_seq - 1, n_seq)
    after = lax.rem(me + 1, n_seq)

    @pl.when(me > 0)
    def _():
        halo(0, before).start()

    @pl.when(me < n_seq - 1)
    def _():
        halo(1, after).start()

    theirs = (1 - mp) * share

    def share_to(index, begin, many):
        return pltpu.make_async_remote_copy(
            src_ref=share_v.at[pl.ds(begin, many)],
            dst_ref=other_v.at[pl.ds(begin, many)],
            send_sem=m_send.at[index],
            recv_sem=m_recv.at[index],
            device_id={"mp": 1 - mp},
            device_id_type=MESH,
        )

    shares = [(t, BORDER + t * TILE, TILE) for t in range(share_tiles)] + [
        (share_tiles, 0, BORDER),
        (share_tiles + 1, BORDER + share, BORDER),
    ]

    def cast_share(begin, many):
        share_v[pl.ds(begin, many), :] = slope_f[
            pl.ds(pl.multiple_of(theirs + begin, BORDER), many), :
        ].astype(BF16)

    for index, begin, many in shares[:share_tiles]:
        cast_share(begin, many)
        share_to(index, begin, many).start()

    def windows(tile):
        at = pl.ds(pl.multiple_of(tile * TILE, TILE), TILE)
        near = slope_f[pl.ds(pl.multiple_of(BORDER - 8 + tile * TILE, 8), TILE + 16), :]
        for tap in range(taps):
            begin = 8 + reach - tap
            wins_v[at, pl.ds(tap * width, width)] = near[begin : begin + TILE].astype(BF16)

    @pl.loop(1, tiles - 1)
    def _(tile):
        windows(tile)

    @pl.when(me < n_seq - 1)
    def _():
        halo(0, before).wait_recv()

    @pl.when(me == n_seq - 1)
    def _():
        slope_f[high, :] = jnp.zeros((8, width), F32)

    @pl.when(me > 0)
    def _():
        halo(1, after).wait_recv()

    @pl.when(me == 0)
    def _():
        slope_f[low, :] = jnp.zeros((8, width), F32)

    slope_f[pl.ds(0, 8), :] = jnp.zeros((8, width), F32)
    slope_f[pl.ds(BORDER + rows_dev + 8, 8), :] = jnp.zeros((8, width), F32)
    for index, begin, many in shares[share_tiles:]:
        cast_share(begin, many)
        share_to(index, begin, many).start()

    windows(0)
    windows(tiles - 1)

    def chunk_at(turn):
        return pl.ds(pl.multiple_of(turn * per_chunk, per_chunk), per_chunk)

    def to_twin(turn, at_core):
        region = (chunk_at(turn), pl.ds(pl.multiple_of((1 - at_core) * half, 16), half))
        return pltpu.make_async_remote_copy(
            src_ref=wb_v.at[region[0], region[1]],
            dst_ref=wa_v.at[region[0]],
            send_sem=a_send.at[turn],
            recv_sem=a_recv.at[turn],
            device_id=at_seq(twin),
            device_id_type=MESH,
        )

    def to_x(turn, step):
        peer = lax.rem(xme + step, n_x)
        return pltpu.make_async_remote_copy(
            src_ref=wsb_v.at[peer, chunk_at(turn)],
            dst_ref=wrb_v.at[step - 1, chunk_at(turn)],
            send_sem=b_send.at[step - 1, turn],
            recv_sem=b_recv.at[step - 1, turn],
            device_id={"batch": peer},
            device_id_type=MESH,
        )

    if block > taps * chip_rows:
        pad = block - taps * chip_rows
        wb_v[:, pl.ds(taps * chip_rows, pad), :] = jnp.zeros((n_chip, pad, width), BF16)

    @pl.loop(0, CHUNKS + 1)
    def _(turn):
        @pl.when(turn < CHUNKS)
        def _():
            lhs = convt_v[pl.ds(pl.multiple_of(turn * chunk_rows, 16), chunk_rows), :]
            product = jnp.dot(lhs, wins_v[...], preferred_element_type=F32)
            for place in range(per_chunk):
                for tap in range(taps):
                    wb_v[turn * per_chunk + place, pl.ds(tap * chip_rows, chip_rows), :] = product[
                        place * chip_rows : (place + 1) * chip_rows,
                        tap * width : (tap + 1) * width,
                    ].astype(BF16)
            to_twin(turn, core).start()

        @pl.when(turn > 0)
        def _():
            last = turn - 1
            to_twin(last, core).wait_recv()
            at = chunk_at(last)
            own_half = pl.multiple_of(core * half, 16)
            for q in range(n_x):
                total = wb_v[at, pl.ds(own_half + q * piece, piece), :].astype(F32) + wa_v[
                    at, pl.ds(q * piece, piece), :
                ].astype(F32)
                wsb_v[q, at] = total.astype(BF16)
            mine = pl.multiple_of(xme * piece, 16)
            wown_v[at] = wb_v[at, pl.ds(own_half + mine, piece), :].astype(F32) + wa_v[
                at, pl.ds(mine, piece), :
            ].astype(F32)
            for step in range(1, n_x):
                to_x(last, step).start()

    for way in range(2):
        kernel_twin(way, 1 - core).wait_recv()
    loads[4].wait()
    for index, begin, many in shares[share_tiles:]:
        share_to(index, begin, many).wait_recv()
        other_f[pl.ds(begin, many), :] = other_v[pl.ds(begin, many), :].astype(F32)
    for index, begin, many in shares[:share_tiles]:
        share_to(index, begin, many).wait_recv()
        other_f[pl.ds(begin, many), :] = other_v[pl.ds(begin, many), :].astype(F32)

    ours = mp * share
    pick = (
        lax.broadcasted_iota(jnp.int32, (TILE // 2, TILE), 1)
        == 2 * lax.broadcasted_iota(jnp.int32, (TILE // 2, TILE), 0)
    )
    pick = jnp.where(pick, 1.0, 0.0).astype(BF16)

    def outs(tile):
        at = pl.ds(pl.multiple_of(tile * TILE, TILE), TILE)
        low_at = pl.ds(pl.multiple_of(tile * (TILE // 2), TILE // 2), TILE // 2)
        return (
            pltpu.make_async_copy(skip_v.at[at], skip_ref.at[at], out_sem.at[tile]),
            pltpu.make_async_copy(
                lower_v.at[low_at], lower_ref.at[low_at], out_sem.at[share_tiles + tile]
            ),
        )

    def input_tile(tile):
        near = pl.multiple_of(BORDER - 8 + tile * TILE, 8)
        mine = slope_f[pl.ds(pl.multiple_of(ours + near, 8), TILE + 16), :]
        other = other_f[pl.ds(near, TILE + 16), :]
        for tap in range(taps):
            begin = 8 + reach - tap
            window = jnp.concatenate(
                [mine[begin : begin + TILE].astype(BF16), other[begin : begin + TILE].astype(BF16)],
                axis=1,
            )
            product = lax.dot_general(
                window, kfull_v[tap], (((1,), (1,)), ((), ())), preferred_element_type=F32
            )
            if tap == 0:
                acc_v[...] = product
            else:
                acc_v[...] += product
        total = acc_v[...]
        paired = (total + pltpu.roll(total, TILE - 1, 0)).astype(BF16)
        at = pl.ds(pl.multiple_of(tile * TILE, TILE), TILE)
        low_at = pl.ds(pl.multiple_of(tile * (TILE // 2), TILE // 2), TILE // 2)
        skip_v[at, :] = total.astype(BF16)
        lower_v[low_at, :] = jnp.dot(pick, paired, preferred_element_type=F32).astype(BF16)
        for copy in outs(tile):
            copy.start()

    def to_chip(target, slot):
        return pltpu.make_async_remote_copy(
            src_ref=wsc_v.at[target],
            dst_ref=wrc_v.at[slot],
            send_sem=c_send.at[slot],
            recv_sem=c_recv.at[slot],
            device_id=at_seq(2 * target + core),
            device_id_type=MESH,
        )

    def x_sum(turn):
        at = chunk_at(turn)
        for step in range(1, n_x):
            to_x(turn, step).wait_recv()
        total = wown_v[at]
        for step in range(1, n_x):
            total = total + wrb_v[step - 1, at].astype(F32)
        wown_v[at] = total
        for i in range(per_chunk):
            target = turn + CHUNKS * i
            wsc_v[target] = total[i].astype(BF16)

            @pl.when(target != chip)
            def _():
                to_chip(target, lax.rem(target - chip + n_chip, n_chip)).start()

    @pl.loop(0, CHUNKS)
    def _(turn):
        @pl.when(turn < share_tiles)
        def _():
            input_tile(turn)

        x_sum(turn)

    own_place = lax.rem(chip, CHUNKS) * per_chunk + chip // CHUNKS
    final = wown_v[own_place]
    for slot in range(1, n_chip):
        to_chip(chip, slot).wait_recv()
        final = final + wrc_v[slot].astype(F32)
    worker = core * n_x + xme
    wfin_v[worker] = final * scale

    def to_worker(index, target):
        return pltpu.make_async_remote_copy(
            src_ref=wfin_v.at[worker],
            dst_ref=wfin_v.at[worker],
            send_sem=d_send.at[index],
            recv_sem=d_recv.at[index],
            device_id=target,
            device_id_type=MESH,
        )

    def from_worker(index, who):
        return pltpu.make_async_remote_copy(
            src_ref=wfin_v.at[worker],
            dst_ref=wfin_v.at[who],
            send_sem=d_send.at[index],
            recv_sem=d_recv.at[index],
            device_id=at_seq(twin),
            device_id_type=MESH,
        )

    for step in range(n_x):
        peer = lax.rem(xme + step, n_x)
        to_worker(step, {"seq": twin, "batch": peer}).start()
        if step:
            to_worker(n_x + step, {"batch": peer}).start()
    for step in range(n_x):
        peer = lax.rem(xme + n_x - step, n_x)
        from_worker(step, (1 - core) * n_x + peer).wait_recv()
        if step:
            from_worker(n_x + step, core * n_x + peer).wait_recv()

    whole = wfin_v[...].reshape(block, width)
    upper = jnp.concatenate(
        [
            whole[tap * chip_rows : tap * chip_rows + chip_rows // 2][None]
            for tap in range(taps)
        ]
    )
    under = jnp.concatenate(
        [
            whole[tap * chip_rows + chip_rows // 2 : (tap + 1) * chip_rows][None]
            for tap in range(taps)
        ]
    )
    weight_ref[...] = jnp.where(core == 0, upper, under)

    for tile in range(share_tiles):
        for copy in outs(tile):
            copy.wait()

    @pl.loop(1, n_seq)
    def _(step):
        offsets_to(step).wait_send()
        grads_to(step).wait_send()

    for way in range(2):
        kernel_across(way, up).wait_send()
        kernel_twin(way, core).wait_send()

    @pl.when(me > 0)
    def _():
        halo(0, before).wait_send()

    @pl.when(me < n_seq - 1)
    def _():
        halo(1, after).wait_send()

    for index, begin, many in shares:
        share_to(index, begin, many).wait_send()
    for turn in range(CHUNKS):
        to_twin(turn, core).wait_send()
        for step in range(1, n_x):
            to_x(turn, step).wait_send()
    for slot in range(1, n_chip):
        to_chip(chip, slot).wait_send()
    for step in range(n_x):
        to_worker(step, at_seq(twin)).wait_send()
        if step:
            to_worker(n_x + step, at_seq(twin)).wait_send()


def shards(
    conv_input, pre_activation, track_gradient, kernel, pair_rows, pair_count, pair_gradient
):
    n_seq, n_x = lax.axis_size("seq"), lax.axis_size("batch")
    rows_dev, width = track_gradient.shape[1:]
    depth = conv_input.shape[2]
    taps = kernel.shape[0]
    pairs = pair_rows.shape[1]
    endpoints = 2 * pairs
    cap = min(endpoints, 6 * pairs // n_seq)
    n_chip = n_seq // 2
    share = rows_dev // 2
    share_tiles = share // TILE
    chip_rows = depth // n_chip
    unit = 32 * n_x
    block = -(-taps * chip_rows // unit) * unit
    half = block // 2
    piece = half // n_x
    scale = (rows_dev * n_seq * n_x) ** -0.5
    sizes = (n_seq, n_x, cap, rows_dev, width, depth, taps, scale)
    any_spec = pl.BlockSpec(memory_space=pl.ANY)
    vmem = pltpu.VMEM
    dma = pltpu.SemaphoreType.DMA
    skip, lower, weight = pl.pallas_call(
        functools.partial(body, sizes),
        out_shape=(
            jax.ShapeDtypeStruct((share, depth), BF16),
            jax.ShapeDtypeStruct((share // 2, depth), BF16),
            jax.ShapeDtypeStruct((taps, chip_rows // 2, width), F32),
        ),
        in_specs=[
            pl.BlockSpec(memory_space=pltpu.VMEM),
            pl.BlockSpec(memory_space=pltpu.SMEM),
        ]
        + [any_spec] * 5,
        out_specs=(any_spec, any_spec, pl.BlockSpec(memory_space=pltpu.VMEM)),
        scratch_shapes=[
            vmem((endpoints, width), BF16),
            vmem((n_seq, endpoints), jnp.int32),
            vmem((PACK * SLOT_ROWS, endpoints), BF16),
            vmem((n_seq, cap, width), BF16),
            vmem((n_seq * cap, width), BF16),
            vmem((n_seq, 8, SLOT_ROWS), F32),
            vmem((n_seq, 8, SLOT_ROWS), F32),
            vmem((rows_dev, width), BF16),
            vmem((rows_dev, width), BF16),
            vmem((rows_dev, depth), BF16),
            vmem((depth, rows_dev), BF16),
            vmem((rows_dev + 2 * BORDER, width), F32),
            vmem((rows_dev, width), F32),
            vmem((taps, depth, 2 * width), BF16),
            vmem((share + 2 * BORDER, width), BF16),
            vmem((share + 2 * BORDER, width), BF16),
            vmem((share + 2 * BORDER, width), F32),
            vmem((rows_dev, taps * width), BF16),
            vmem((TILE, depth), F32),
            vmem((n_chip, block, width), BF16),
            vmem((n_chip, half, width), BF16),
            vmem((n_x, n_chip, piece, width), BF16),
            vmem((n_x - 1, n_chip, piece, width), BF16),
            vmem((n_chip, piece, width), F32),
            vmem((n_chip, piece, width), BF16),
            vmem((n_chip, piece, width), BF16),
            vmem((2 * n_x, piece, width), F32),
            vmem((share, depth), BF16),
            vmem((share // 2, depth), BF16),
            dma((5,)),
            dma((n_seq,)),
            dma((n_seq,)),
            dma((n_seq,)),
            dma((n_seq,)),
            dma((2,)),
            dma((2,)),
            dma((2,)),
            dma((2,)),
            dma((2,)),
            dma((2,)),
            dma((share_tiles + 2,)),
            dma((share_tiles + 2,)),
            dma((CHUNKS,)),
            dma((CHUNKS,)),
            dma((n_x - 1, CHUNKS)),
            dma((n_x - 1, CHUNKS)),
            dma((n_chip,)),
            dma((n_chip,)),
            dma((2 * n_x,)),
            dma((2 * n_x,)),
            dma((2 * share_tiles,)),
        ],
        compiler_params=pltpu.CompilerParams(
            collective_id=0, has_side_effects=True, vmem_limit_bytes=63 * 1024 * 1024
        ),
    )(
        pair_rows[0].reshape(1, endpoints),
        pair_count,
        pair_gradient[0].reshape(endpoints, width),
        track_gradient[0],
        pre_activation[0],
        conv_input[0],
        kernel,
    )
    return skip[None], lower[None], weight


def solution(mesh):
    in_specs = (
        P("batch", "seq", None),
        P("batch", "seq", "mp"),
        P("batch", "seq", "mp"),
        P(None, None, "mp"),
        P("batch", "seq", None),
        P("batch", "seq"),
        P("batch", "seq", None, "mp"),
    )
    out_specs = (
        P("batch", ("seq", "mp"), None),
        P("batch", ("seq", "mp"), None),
        P(None, "seq", "mp"),
    )
    return jax.shard_map(shards, mesh=mesh, in_specs=in_specs, out_specs=out_specs, check_vma=False)
```

time: 1460 us -> 135 us (0.09)
  waiting for transfers between devices: 1300 us -> 0 us
  Pallas kernels: 0 us -> 123 us
  other arithmetic: 58.6 us -> 0 us
  matrix products: 33.9 us -> 0 us
  starting transfers between devices: 30.4 us -> 0 us
  between operations: 16.3 us -> 1.3 us
    psum x1 -> x0, waiting for transfers between devices: 1250 us -> none  [shards(): summed = lax.psum(kernel_local, ('seq', 'batch'))]
    pallas_call x0 -> x1, Pallas kernels: none -> 123 us  [shards(): pl.pallas_call(functools.partial(body, sizes), out_shape=(jax.ShapeDtypeS...]
    all_to_all x2 -> x0, waiting for transfers between devices: 52.1 us -> none  [the longest x1 52.1 us: shards(): lax.all_to_all(send_grads.reshape(seq_count, capacity, width_local), 'seq...]
    dot_general x10 -> x0, matrix products: 33.9 us -> none  [the longest x5 21.6 us: conv_rows(): lax.dot_general(window_rows, kernel_part[position], (((1,), (1,)), ((), (...]
    scatter-add x1 -> x0, other arithmetic: 22.8 us -> none  [shards(): out_grad = track_gradient[0].astype(jnp.float32).at[got_offsets.reshape(s...]
    all_to_all x2 -> x0, starting transfers between devices: 22.6 us -> none  [the longest x1 12.8 us: shards(): lax.all_to_all(send_offsets.reshape(seq_count, capacity), 'seq', split_ax...]
  transfers between devices with their start and end apart: 6 -> 0, of which waited for: 2 -> 0; matrix products, arithmetic and copies ran while one was open for 3% -> 0% of each run, Pallas kernels for 0% -> 0%
where the time goes in v2:
time: 135 us; the launch traced here: 133 us
  Pallas kernels  123 us (91%)
  local copies, waits for them, and re-layouts  9.05 us (7%)
    pallas_call x1, Pallas kernels, shards(): pl.pallas_call(functools.partial(body, sizes), out_shape=(jax.ShapeDtypeS...  123 us
    unnamed x8, local copies, waits for them, and re-layouts  5.31 us
    another operation x1, local copies, waits for them, and re-layouts, shards(): pair_gradient[0].reshape(endpoints, width)  2.95 us

profile of v2, /device:TPU:1, one launch (start us, length us, event | category | flops | bytes accessed | tf_op | source)
XLA Modules:
  0.0 132.9 jit_solution(17664528429440322914)
XLA Ops:
  1.3 0.8 copy.11
  2.1 0.8 reshape_squeeze.6.rows_ref
  2.9 3.0 %reshape_squeeze.7.pairs_ref = bf16[1024,384]{1,0:T(8,128)(2,1)} reshape(bf16[1,512,2,384]{3,2,1,0:T(2,128)(2,1)} %param.13) | data formatting | bytes 1572864 | tf_op jit(solution)/shard_map/reshape;squeeze | solution.py:693
  5.8 122.6 %shard_map.94 = (bf16[1024,768]{1,0:T(8,128)(2,1)}, bf16[512,768]{1,0:T(8,128)(2,1)}, f32[5,24,384]{2,1,0:T(8,128)}) custom-call(s32[1,1024]{1,0:T(1,128)} %reshape_squeeze.6.rows_ref, s32[1,1]{1,0:T(1,128)S(6)} %copy.15.count_ref, bf16[1024,384]{1,0:T(8,128)(2,1)} %reshape_squeeze.7.pairs_ref, bf16[2048,384]{1,0:T(8,128)(2,1)} %bitcast.6, ...), custom_call_target="tpu_custom_call" | custom-call | tf_op jit(solution)/shard_map/pallas_call | solution.py:621
  128.4 0.0 copy-start
  128.4 2.7 %copy.16 = bf16[1,1024,768]{2,1,0:T(8,128)(2,1)} copy(bf16[1,1024,768]{2,1,0:T(8,128)(2,1)} %bitcast.8) | data formatting | bytes 3145728
  131.2 0.0 copy-done
  131.2 0.0 copy-start.1
  131.2 0.9 copy.17
  132.0 0.2 copy-done.1
  132.3 0.7 copy.18
Async XLA Ops:
  128.4 2.7 %copy-start = (bf16[512,768]{1,0:T(8,128)(2,1)S(1)}, bf16[512,768]{1,0:T(8,128)(2,1)}, u32[]{:S(2)}) copy-start(bf16[512,768]{1,0:T(8,128)(2,1)} %get-tuple-element.7) | copy-start | bytes 2359300
  131.2 1.1 copy-start.1

commit v3 on v2

v3 whole, which is shorter than its diff:
```python
import functools

import jax
import jax.numpy as jnp
from jax import lax
from jax.experimental import pallas as pl
from jax.experimental.pallas import tpu as pltpu
from jax.sharding import PartitionSpec as P

MESH = pl.DeviceIdType.MESH
F32 = jnp.float32
BF16 = jnp.bfloat16
root_half = 0.7071067811865476
inv_root_tau = 0.3989422804014327
TILE = 256
BORDER = 16
CHUNKS = 4
PACK = 4
SLOT_ROWS = 128
LANES = ((0, 256), (256, 128))


def gelu_slope(values):
    normal_cdf = 0.5 * (1.0 + lax.erf(values * root_half))
    return normal_cdf + values * inv_root_tau * jnp.exp(-0.5 * values * values)


def body(
    sizes,
    rows_ref, count_ref, pairs_ref, track_ref, pre_ref, conv_ref, kern_ref,
    skip_ref, lower_ref, weight_ref,
    raw_v, pairs_v, slot_v, onehot_v, send_v, recv_v, soff_v, roff_v,
    track_v, pre_v, conv_v, convt_v, slope_f, grad_v, kfull_v,
    share_v, other_v, other_f, wins_v, acc_v,
    wb_v, wa_v, wsb_v, wrb_v, wown_v, wsc_v, wrc_v, wfin_v,
    skip_v, lower_v,
    load_sem, g_send, g_recv, o_send, o_recv, kx_send, kx_recv, kc_send, kc_recv,
    h_send, h_recv, m_send, m_recv, a_send, a_recv, b_send, b_recv,
    c_send, c_recv, d_send, d_recv, out_sem,
):
    n_seq, n_x, cap, rows_dev, width, depth, taps, scale = sizes
    n_chip = n_seq // 2
    n_z = n_chip // 2
    reach = taps // 2
    endpoints = 2 * pairs_ref.shape[0]
    share = rows_dev // 2
    tiles = rows_dev // TILE
    share_tiles = share // TILE
    chip_rows = depth // n_chip
    block = wb_v.shape[1]
    half = block // 2
    piece = half // n_x
    per_chunk = n_chip // CHUNKS
    chunk_rows = chip_rows * per_chunk
    quarter = depth // 4

    me = lax.axis_index("seq")
    mp = lax.axis_index("mp")
    xme = lax.axis_index("batch")
    core = lax.rem(me, 2)
    chip = me // 2
    yhi = chip // n_z
    zme = lax.rem(chip, n_z)
    twin = me + 1 - 2 * core

    def at_seq(target):
        return {"seq": target}

    up = {"seq": (lax.rem(yhi + mp, 2) * n_z + zme) * 2 + core, "mp": 1 - mp}
    down = {"seq": (lax.rem(yhi + 1 - mp, 2) * n_z + zme) * 2 + core, "mp": 1 - mp}

    loads = [
        pltpu.make_async_copy(pairs_ref, raw_v, load_sem.at[0]),
        pltpu.make_async_copy(pre_ref, pre_v, load_sem.at[1]),
        pltpu.make_async_copy(track_ref, track_v, load_sem.at[2]),
        pltpu.make_async_copy(conv_ref, conv_v, load_sem.at[3]),
    ] + [
        pltpu.make_async_copy(
            kern_ref.at[:, :, pl.ds(lane, many)],
            kfull_v.at[:, :, pl.ds(2 * lane, many)],
            load_sem.at[4 + part],
        )
        for part, (lane, many) in enumerate(LANES)
    ]
    for load in loads:
        load.start()

    barrier = pltpu.get_barrier_semaphore()

    def greet(target):
        pl.semaphore_signal(barrier, inc=1, device_id=target, device_id_type=MESH)

    @pl.loop(1, n_seq)
    def _(step):
        greet(at_seq(lax.rem(me + step, n_seq)))

    @pl.loop(1, n_x)
    def _(step):
        peer = lax.rem(xme + step, n_x)
        greet({"batch": peer})
        greet({"seq": twin, "batch": peer})

    greet(up)
    greet(down)

    lane = lax.broadcasted_iota(jnp.int32, (1, endpoints), 1)
    rows = rows_ref[...]
    owner = rows // rows_dev
    offset = rows - owner * rows_dev
    owner = jnp.where(lane // 2 < count_ref[0, 0], owner, n_seq)
    hit = owner == lax.broadcasted_iota(jnp.int32, (n_seq, endpoints), 0)
    rank = hit.astype(jnp.int32)
    wide_lane = lax.broadcasted_iota(jnp.int32, (n_seq, endpoints), 1)
    shift = 1
    while shift < endpoints:
        rank = rank + jnp.where(wide_lane >= shift, pltpu.roll(rank, shift, 1), 0)
        shift *= 2
    slot_v[...] = jnp.where(hit, rank - 1, -1)
    kind = lax.broadcasted_iota(jnp.int32, (16, endpoints), 0)
    parts = jnp.where(kind == 0, offset // 64, jnp.where(kind == 1, lax.rem(offset, 64), 1))
    parts = parts.astype(F32).astype(BF16)

    loads[0].wait()
    pairs_v[...] = raw_v[...].reshape(endpoints, width)
    pl.semaphore_wait(barrier, (n_seq - 1) + 2 * (n_x - 1) + 2)

    def grads_to(part, step):
        lanes = pl.ds(*LANES[part])
        return pltpu.make_async_remote_copy(
            src_ref=send_v.at[step, :, lanes],
            dst_ref=recv_v.at[pl.ds(pl.multiple_of(step * cap, 16), cap), lanes],
            send_sem=g_send.at[part, step],
            recv_sem=g_recv.at[part, step],
            device_id=at_seq(lax.rem(me + step, n_seq)),
            device_id_type=MESH,
        )

    def offsets_to(step):
        return pltpu.make_async_remote_copy(
            src_ref=soff_v.at[step],
            dst_ref=roff_v.at[step],
            send_sem=o_send.at[step],
            recv_sem=o_recv.at[step],
            device_id=at_seq(lax.rem(me + step, n_seq)),
            device_id_type=MESH,
        )

    def pack(first):
        for i in range(PACK):
            target = lax.rem(me + first + i, n_seq)
            slots = slot_v[pl.ds(target, 1), :].astype(F32).astype(BF16)
            places = lax.broadcasted_iota(jnp.int32, (SLOT_ROWS, endpoints), 0)
            onehot_v[pl.ds(i * SLOT_ROWS, SLOT_ROWS), :] = jnp.where(
                slots == places.astype(F32).astype(BF16), jnp.ones((), BF16), jnp.zeros((), BF16)
            )
        onehot = onehot_v[...]
        listed = jnp.dot(onehot, pairs_v[...], preferred_element_type=F32).astype(BF16)
        marks = lax.dot_general(
            parts, onehot, (((1,), (1,)), ((), ())), preferred_element_type=F32
        )
        where_to = jnp.where(marks[2:3] > 0.5, marks[0:1] * 64.0 + marks[1:2], -1.0)
        return listed, where_to

    def emit(first, begin):
        listed, where_to = pack(first)
        for i in range(PACK):
            some = listed[i * SLOT_ROWS : i * SLOT_ROWS + cap]
            place = where_to[:, i * SLOT_ROWS : (i + 1) * SLOT_ROWS]
            if i < begin:
                recv_v[pl.ds(0, cap), :] = some
                roff_v[0] = place
            else:
                send_v[first + i] = some
                soff_v[first + i] = place
                offsets_to(first + i).start()
                grads_to(0, first + i).start()

    def kernel_piece(index):
        return pl.ds(pl.multiple_of(index * quarter, 16), quarter)

    def kernel_across(way, part, target):
        lane, many = LANES[part]
        rows_at = kernel_piece(2 * core + way)
        return pltpu.make_async_remote_copy(
            src_ref=kern_ref.at[:, rows_at, pl.ds(lane, many)],
            dst_ref=kfull_v.at[:, rows_at, pl.ds(2 * lane + many, many)],
            send_sem=kx_send.at[way, part],
            recv_sem=kx_recv.at[way, part],
            device_id=target,
            device_id_type=MESH,
        )

    def kernel_twin(way, part, at_core):
        lane, many = LANES[part]
        region = kfull_v.at[:, kernel_piece(2 * at_core + way), pl.ds(2 * lane + many, many)]
        return pltpu.make_async_remote_copy(
            src_ref=region,
            dst_ref=region,
            send_sem=kc_send.at[way, part],
            recv_sem=kc_recv.at[way, part],
            device_id=at_seq(twin),
            device_id_type=MESH,
        )

    halves = [(way, part) for part in range(len(LANES)) for way in range(2)]
    for way, part in halves:
        kernel_across(way, part, down if way else up).start()

    emit(0, 1)

    @pl.loop(1, n_seq // PACK)
    def _(turn):
        emit(turn * PACK, 0)

    for part in range(1, len(LANES)):

        @pl.loop(1, n_seq)
        def _(step):
            grads_to(part, step).start()

    loads[1].wait()
    loads[2].wait()

    @pl.loop(0, tiles)
    def _(tile):
        at = pl.ds(pl.multiple_of(tile * TILE, TILE), TILE)
        grad_v[at, :] = gelu_slope(pre_v[at, :].astype(F32))
        slope_f[pl.ds(pl.multiple_of(BORDER + tile * TILE, BORDER), TILE), :] = track_v[
            at, :
        ].astype(F32)

    loads[3].wait()

    @pl.loop(0, tiles)
    def _(tile):
        at = pl.ds(pl.multiple_of(tile * TILE, TILE), TILE)
        turned = conv_v[at, :].T
        for place in range(n_chip):
            source = place // per_chunk + CHUNKS * (place % per_chunk)
            convt_v[pl.ds(place * chip_rows, chip_rows), at] = turned[
                source * chip_rows : (source + 1) * chip_rows
            ]

    tile_lane = lax.broadcasted_iota(jnp.int32, (1, SLOT_ROWS), 1)

    def four_lists(first):
        p = [roff_v[first + i] for i in range(4)]
        one = pltpu.roll(p[1], 96, 1)
        two = pltpu.roll(p[2], 64, 1)
        three = pltpu.roll(p[3], 32, 1)
        return jnp.concatenate(
            [
                jnp.where(tile_lane < 96, p[0], one),
                jnp.where(tile_lane < 64, one, two),
                jnp.where(tile_lane < 32, two, three),
            ],
            axis=1,
        )

    groups = [(first, 8) for first in range(0, n_seq - 8, 8)] + [(n_seq - 8, 4), (n_seq - 4, 4)]
    before = lax.rem(me + n_seq - 1, n_seq)
    after = lax.rem(me + 1, n_seq)
    low = pl.ds(BORDER - 8, 8)
    high = pl.ds(BORDER + rows_dev, 8)
    theirs = (1 - mp) * share
    ours = mp * share
    last_part = len(LANES) - 1

    few_rows = lax.broadcasted_iota(jnp.int32, (16, 8 * cap), 0).astype(F32).astype(BF16)
    one, zero = jnp.ones((), BF16), jnp.zeros((), BF16)

    def junction(part, begin_group, end_group):
        lanes = pl.ds(*LANES[part])
        for first, many in groups[begin_group:end_group]:
            @pl.loop(max(first, 1), first + many)
            def _(step):
                if part == 0:
                    offsets_to(step).wait_recv()
                grads_to(part, step).wait_recv()

            lists = jnp.concatenate([four_lists(first + i) for i in range(0, many, 4)], axis=1)
            ends = first + many == n_seq

            @pl.loop(0, tiles)
            def _(tile, first=first, many=many, lists=lists, ends=ends):
                wanted = (lists - (tile * TILE).astype(F32)).astype(BF16)
                wanted = jnp.broadcast_to(wanted, (16, many * cap))
                onehot = jnp.concatenate(
                    [
                        jnp.where(wanted == few_rows[:, : many * cap] + 16.0 * i, one, zero)
                        for i in range(TILE // 16)
                    ]
                )
                at = pl.ds(pl.multiple_of(BORDER + tile * TILE, BORDER), TILE)
                total = slope_f[at, lanes] + jnp.dot(
                    onehot,
                    recv_v[pl.ds(first * cap, many * cap), lanes],
                    preferred_element_type=F32,
                )
                if ends:
                    slope = grad_v[pl.ds(pl.multiple_of(tile * TILE, TILE), TILE), lanes]
                    total = (total * slope).astype(BF16).astype(F32)
                slope_f[at, lanes] = total

    def halo(part, way, target):
        lanes = pl.ds(*LANES[part])
        own = pl.ds(BORDER, 8) if way == 0 else pl.ds(BORDER + rows_dev - 8, 8)
        return pltpu.make_async_remote_copy(
            src_ref=slope_f.at[own, lanes],
            dst_ref=slope_f.at[high if way == 0 else low, lanes],
            send_sem=h_send.at[part, way],
            recv_sem=h_recv.at[part, way],
            device_id=at_seq(target),
            device_id_type=MESH,
        )

    def share_to(part, index, begin, many):
        lanes = pl.ds(*LANES[part])
        return pltpu.make_async_remote_copy(
            src_ref=share_v.at[pl.ds(begin, many), lanes],
            dst_ref=other_v.at[pl.ds(begin, many), lanes],
            send_sem=m_send.at[part, index],
            recv_sem=m_recv.at[part, index],
            device_id={"mp": 1 - mp},
            device_id_type=MESH,
        )

    shares = [(t, BORDER + t * TILE, TILE) for t in range(share_tiles)] + [
        (share_tiles, 0, BORDER),
        (share_tiles + 1, BORDER + share, BORDER),
    ]

    def send_share(part, index, begin, many):
        lanes = pl.ds(*LANES[part])
        share_v[pl.ds(begin, many), lanes] = slope_f[
            pl.ds(pl.multiple_of(theirs + begin, BORDER), many), lanes
        ].astype(BF16)
        share_to(part, index, begin, many).start()

    def windows(part, tile):
        lane, many = LANES[part]
        at = pl.ds(pl.multiple_of(tile * TILE, TILE), TILE)
        near = slope_f[
            pl.ds(pl.multiple_of(BORDER - 8 + tile * TILE, 8), TILE + 16), pl.ds(lane, many)
        ]
        for tap in range(taps):
            begin = 8 + reach - tap
            wins_v[at, pl.ds(taps * lane + tap * many, many)] = near[
                begin : begin + TILE
            ].astype(BF16)

    def slopes_inner(part):
        @pl.when(me > 0)
        def _():
            halo(part, 0, before).start()

        @pl.when(me < n_seq - 1)
        def _():
            halo(part, 1, after).start()

        for index, begin, rows_many in shares[:share_tiles]:
            send_share(part, index, begin, rows_many)

        @pl.loop(1, tiles - 1)
        def _(tile):
            windows(part, tile)

    def slopes_outer(part):
        lanes = pl.ds(*LANES[part])
        many = LANES[part][1]

        @pl.when(me < n_seq - 1)
        def _():
            halo(part, 0, before).wait_recv()

        @pl.when(me == n_seq - 1)
        def _():
            slope_f[high, lanes] = jnp.zeros((8, many), F32)

        @pl.when(me > 0)
        def _():
            halo(part, 1, after).wait_recv()

        @pl.when(me == 0)
        def _():
            slope_f[low, lanes] = jnp.zeros((8, many), F32)

        for index, begin, rows_many in shares[share_tiles:]:
            send_share(part, index, begin, rows_many)
        windows(part, 0)
        windows(part, tiles - 1)

    def chunk_at(turn):
        return pl.ds(pl.multiple_of(turn * per_chunk, per_chunk), per_chunk)

    def to_twin(part, turn, at_core):
        lanes = pl.ds(*LANES[part])
        half_at = pl.ds(pl.multiple_of((1 - at_core) * half, 16), half)
        return pltpu.make_async_remote_copy(
            src_ref=wb_v.at[chunk_at(turn), half_at, lanes],
            dst_ref=wa_v.at[chunk_at(turn), :, lanes],
            send_sem=a_send.at[part, turn],
            recv_sem=a_recv.at[part, turn],
            device_id=at_seq(twin),
            device_id_type=MESH,
        )

    def to_x(part, turn, step):
        lanes = pl.ds(*LANES[part])
        peer = lax.rem(xme + step, n_x)
        return pltpu.make_async_remote_copy(
            src_ref=wsb_v.at[peer, chunk_at(turn), :, lanes],
            dst_ref=wrb_v.at[step - 1, chunk_at(turn), :, lanes],
            send_sem=b_send.at[part, step - 1, turn],
            recv_sem=b_recv.at[part, step - 1, turn],
            device_id={"batch": peer},
            device_id_type=MESH,
        )

    if block > taps * chip_rows:
        pad = block - taps * chip_rows
        wb_v[:, pl.ds(taps * chip_rows, pad), :] = jnp.zeros((n_chip, pad, width), BF16)

    def weights(part):
        lane, many = LANES[part]
        lanes = pl.ds(lane, many)

        @pl.loop(0, CHUNKS)
        def _(turn):
            lhs = convt_v[pl.ds(pl.multiple_of(turn * chunk_rows, 16), chunk_rows), :]
            product = jnp.dot(
                lhs,
                wins_v[:, pl.ds(taps * lane, taps * many)],
                preferred_element_type=F32,
            )
            for place in range(per_chunk):
                for tap in range(taps):
                    wb_v[turn * per_chunk + place, pl.ds(tap * chip_rows, chip_rows), lanes] = (
                        product[
                            place * chip_rows : (place + 1) * chip_rows,
                            tap * many : (tap + 1) * many,
                        ].astype(BF16)
                    )
            to_twin(part, turn, core).start()

    def twin_sum(part):
        lanes = pl.ds(*LANES[part])

        @pl.loop(0, CHUNKS)
        def _(turn):
            to_twin(part, turn, core).wait_recv()
            at = chunk_at(turn)
            own_half = pl.multiple_of(core * half, 16)
            for q in range(n_x):
                total = wb_v[at, pl.ds(own_half + q * piece, piece), lanes].astype(F32) + wa_v[
                    at, pl.ds(q * piece, piece), lanes
                ].astype(F32)
                wsb_v[q, at, :, lanes] = total.astype(BF16)
            for step in range(1, n_x):
                to_x(part, turn, step).start()
            mine = pl.multiple_of(xme * piece, 16)
            wown_v[at, :, lanes] = wb_v[at, pl.ds(own_half + mine, piece), lanes].astype(
                F32
            ) + wa_v[at, pl.ds(mine, piece), lanes].astype(F32)

    pick = (
        lax.broadcasted_iota(jnp.int32, (TILE // 2, TILE), 1)
        == 2 * lax.broadcasted_iota(jnp.int32, (TILE // 2, TILE), 0)
    )
    pick = jnp.where(pick, 1.0, 0.0).astype(BF16)

    def outs(tile):
        at = pl.ds(pl.multiple_of(tile * TILE, TILE), TILE)
        low_at = pl.ds(pl.multiple_of(tile * (TILE // 2), TILE // 2), TILE // 2)
        return (
            pltpu.make_async_copy(skip_v.at[at], skip_ref.at[at], out_sem.at[tile]),
            pltpu.make_async_copy(
                lower_v.at[low_at], lower_ref.at[low_at], out_sem.at[share_tiles + tile]
            ),
        )

    def take_shares(part):
        lanes = pl.ds(*LANES[part])
        for index, begin, many in shares:
            share_to(part, index, begin, many).wait_recv()
            other_f[pl.ds(begin, many), lanes] = other_v[pl.ds(begin, many), lanes].astype(F32)

    def input_tile(part, tile):
        lane, many = LANES[part]
        lanes = pl.ds(lane, many)
        near = pl.multiple_of(BORDER - 8 + tile * TILE, 8)
        at = pl.ds(pl.multiple_of(tile * TILE, TILE), TILE)
        mine = slope_f[pl.ds(pl.multiple_of(ours + near, 8), TILE + 16), lanes]
        other = other_f[pl.ds(near, TILE + 16), lanes]
        for tap in range(taps):
            begin = 8 + reach - tap
            window = jnp.concatenate(
                [mine[begin : begin + TILE].astype(BF16), other[begin : begin + TILE].astype(BF16)],
                axis=1,
            )
            product = lax.dot_general(
                window,
                kfull_v[tap, :, pl.ds(2 * lane, 2 * many)],
                (((1,), (1,)), ((), ())),
                preferred_element_type=F32,
            )
            if part == 0 and tap == 0:
                acc_v[at, :] = product
            else:
                acc_v[at, :] += product
        if part == last_part:
            total = acc_v[at, :]
            paired = (total + pltpu.roll(total, TILE - 1, 0)).astype(BF16)
            low_at = pl.ds(pl.multiple_of(tile * (TILE // 2), TILE // 2), TILE // 2)
            skip_v[at, :] = total.astype(BF16)
            lower_v[low_at, :] = jnp.dot(pick, paired, preferred_element_type=F32).astype(BF16)
            for copy in outs(tile):
                copy.start()

    def to_chip(part, target, slot):
        lanes = pl.ds(*LANES[part])
        return pltpu.make_async_remote_copy(
            src_ref=wsc_v.at[target, :, lanes],
            dst_ref=wrc_v.at[slot, :, lanes],
            send_sem=c_send.at[part, slot],
            recv_sem=c_recv.at[part, slot],
            device_id=at_seq(2 * target + core),
            device_id_type=MESH,
        )

    def x_sum(part, turn):
        lanes = pl.ds(*LANES[part])
        at = chunk_at(turn)
        for step in range(1, n_x):
            to_x(part, turn, step).wait_recv()
        total = wown_v[at, :, lanes]
        for step in range(1, n_x):
            total = total + wrb_v[step - 1, at, :, lanes].astype(F32)
        wown_v[at, :, lanes] = total
        for i in range(per_chunk):
            target = turn + CHUNKS * i
            wsc_v[target, :, lanes] = total[i].astype(BF16)

            @pl.when(target != chip)
            def _():
                to_chip(part, target, lax.rem(target - chip + n_chip, n_chip)).start()

    junction(0, 0, 5)
    slopes_inner(0)
    junction(1, 0, 1)
    slopes_outer(0)
    weights(0)
    for way, part in halves:
        kernel_across(way, part, up).wait_recv()
        kernel_twin(way, part, core).start()
    junction(1, 1, 2)
    twin_sum(0)
    junction(1, 2, 5)
    slopes_inner(1)

    @pl.loop(0, CHUNKS)
    def _(turn):
        x_sum(0, turn)

    slopes_outer(1)
    weights(1)
    twin_sum(1)
    for way, part in halves:
        kernel_twin(way, part, 1 - core).wait_recv()
    loads[4].wait()
    loads[5].wait()
    take_shares(0)

    @pl.loop(0, share_tiles)
    def _(tile):
        input_tile(0, tile)

    @pl.loop(0, CHUNKS)
    def _(turn):
        x_sum(1, turn)

    take_shares(1)

    @pl.loop(0, share_tiles)
    def _(tile):
        input_tile(1, tile)

    own_place = lax.rem(chip, CHUNKS) * per_chunk + chip // CHUNKS
    final = wown_v[own_place]
    for slot in range(1, n_chip):
        for part in range(len(LANES)):
            to_chip(part, chip, slot).wait_recv()
        final = final + wrc_v[slot].astype(F32)
    worker = core * n_x + xme
    wfin_v[worker] = final * scale

    def to_worker(index, target):
        return pltpu.make_async_remote_copy(
            src_ref=wfin_v.at[worker],
            dst_ref=wfin_v.at[worker],
            send_sem=d_send.at[index],
            recv_sem=d_recv.at[index],
            device_id=target,
            device_id_type=MESH,
        )

    def from_worker(index, who):
        return pltpu.make_async_remote_copy(
            src_ref=wfin_v.at[worker],
            dst_ref=wfin_v.at[who],
            send_sem=d_send.at[index],
            recv_sem=d_recv.at[index],
            device_id=at_seq(twin),
            device_id_type=MESH,
        )

    for step in range(n_x):
        peer = lax.rem(xme + step, n_x)
        to_worker(step, {"seq": twin, "batch": peer}).start()
        if step:
            to_worker(n_x + step, {"batch": peer}).start()
    for step in range(n_x):
        peer = lax.rem(xme + n_x - step, n_x)
        from_worker(step, (1 - core) * n_x + peer).wait_recv()
        if step:
            from_worker(n_x + step, core * n_x + peer).wait_recv()

    whole = wfin_v[...].reshape(block, width)
    upper = jnp.concatenate(
        [
            whole[tap * chip_rows : tap * chip_rows + chip_rows // 2][None]
            for tap in range(taps)
        ]
    )
    under = jnp.concatenate(
        [
            whole[tap * chip_rows + chip_rows // 2 : (tap + 1) * chip_rows][None]
            for tap in range(taps)
        ]
    )
    weight_ref[...] = jnp.where(core == 0, upper, under)

    for tile in range(share_tiles):
        for copy in outs(tile):
            copy.wait()

    @pl.loop(1, n_seq)
    def _(step):
        offsets_to(step).wait_send()
        for part in range(len(LANES)):
            grads_to(part, step).wait_send()

    for way, part in halves:
        kernel_across(way, part, up).wait_send()
        kernel_twin(way, part, core).wait_send()
    for part in range(len(LANES)):

        @pl.when(me > 0)
        def _():
            halo(part, 0, before).wait_send()

        @pl.when(me < n_seq - 1)
        def _():
            halo(part, 1, after).wait_send()

        for index, begin, many in shares:
            share_to(part, index, begin, many).wait_send()
        for turn in range(CHUNKS):
            to_twin(part, turn, core).wait_send()
            for step in range(1, n_x):
                to_x(part, turn, step).wait_send()
        for slot in range(1, n_chip):
            to_chip(part, chip, slot).wait_send()
    for step in range(n_x):
        to_worker(step, at_seq(twin)).wait_send()
        if step:
            to_worker(n_x + step, at_seq(twin)).wait_send()


def hand_over(skip_ref, lower_ref, weight_ref, skip_out, lower_out, weight_out):
    skip_out[...] = skip_ref[...]
    lower_out[...] = lower_ref[...]
    weight_out[...] = weight_ref[...]


def shards(
    conv_input, pre_activation, track_gradient, kernel, pair_rows, pair_count, pair_gradient
):
    n_seq, n_x = lax.axis_size("seq"), lax.axis_size("batch")
    rows_dev, width = track_gradient.shape[1:]
    depth = conv_input.shape[2]
    taps = kernel.shape[0]
    pairs = pair_rows.shape[1]
    endpoints = 2 * pairs
    cap = min(endpoints, 6 * pairs // n_seq)
    n_chip = n_seq // 2
    share = rows_dev // 2
    share_tiles = share // TILE
    chip_rows = depth // n_chip
    unit = 32 * n_x
    block = -(-taps * chip_rows // unit) * unit
    half = block // 2
    piece = half // n_x
    scale = (rows_dev * n_seq * n_x) ** -0.5
    sizes = (n_seq, n_x, cap, rows_dev, width, depth, taps, scale)
    any_spec = pl.BlockSpec(memory_space=pl.ANY)
    vmem = pltpu.VMEM
    dma = pltpu.SemaphoreType.DMA
    skip, lower, weight = pl.pallas_call(
        functools.partial(body, sizes),
        out_shape=(
            jax.ShapeDtypeStruct((share, depth), BF16),
            jax.ShapeDtypeStruct((share // 2, depth), BF16),
            jax.ShapeDtypeStruct((taps, chip_rows // 2, width), F32),
        ),
        in_specs=[
            pl.BlockSpec(memory_space=pltpu.VMEM),
            pl.BlockSpec(memory_space=pltpu.SMEM),
        ]
        + [any_spec] * 5,
        out_specs=(any_spec, any_spec, pl.BlockSpec(memory_space=pltpu.VMEM)),
        scratch_shapes=[
            vmem((pairs, 2, width), BF16),
            vmem((endpoints, width), BF16),
            vmem((n_seq, endpoints), jnp.int32),
            vmem((PACK * SLOT_ROWS, endpoints), BF16),
            vmem((n_seq, cap, width), BF16),
            vmem((n_seq * cap, width), BF16),
            vmem((n_seq, 1, SLOT_ROWS), F32),
            vmem((n_seq, 1, SLOT_ROWS), F32),
            vmem((rows_dev, width), BF16),
            vmem((rows_dev, width), BF16),
            vmem((rows_dev, depth), BF16),
            vmem((depth, rows_dev), BF16),
            vmem((rows_dev + 2 * BORDER, width), F32),
            vmem((rows_dev, width), F32),
            vmem((taps, depth, 2 * width), BF16),
            vmem((share + 2 * BORDER, width), BF16),
            vmem((share + 2 * BORDER, width), BF16),
            vmem((share + 2 * BORDER, width), F32),
            vmem((rows_dev, taps * width), BF16),
            vmem((share, depth), F32),
            vmem((n_chip, block, width), BF16),
            vmem((n_chip, half, width), BF16),
            vmem((n_x, n_chip, piece, width), BF16),
            vmem((n_x - 1, n_chip, piece, width), BF16),
            vmem((n_chip, piece, width), F32),
            vmem((n_chip, piece, width), BF16),
            vmem((n_chip, piece, width), BF16),
            vmem((2 * n_x, piece, width), F32),
            vmem((share, depth), BF16),
            vmem((share // 2, depth), BF16),
            dma((6,)),
            dma((2, n_seq)),
            dma((2, n_seq)),
            dma((n_seq,)),
            dma((n_seq,)),
            dma((2, 2)),
            dma((2, 2)),
            dma((2, 2)),
            dma((2, 2)),
            dma((2, 2)),
            dma((2, 2)),
            dma((2, share_tiles + 2)),
            dma((2, share_tiles + 2)),
            dma((2, CHUNKS)),
            dma((2, CHUNKS)),
            dma((2, n_x - 1, CHUNKS)),
            dma((2, n_x - 1, CHUNKS)),
            dma((2, n_chip)),
            dma((2, n_chip)),
            dma((2 * n_x,)),
            dma((2 * n_x,)),
            dma((2 * share_tiles,)),
        ],
        compiler_params=pltpu.CompilerParams(
            collective_id=0, has_side_effects=True, vmem_limit_bytes=63 * 1024 * 1024
        ),
    )(
        pair_rows[0].reshape(1, endpoints),
        pair_count,
        pair_gradient[0],
        track_gradient[0],
        pre_activation[0],
        conv_input[0],
        kernel,
    )
    steps = 4
    specs = (
        pl.BlockSpec((share // steps, depth), lambda i: (i, 0)),
        pl.BlockSpec((share // 2 // steps, depth), lambda i: (i, 0)),
        pl.BlockSpec((taps, chip_rows // 2, width), lambda i: (0, 0, 0)),
    )
    skip, lower, weight = pl.pallas_call(
        hand_over,
        grid=(steps,),
        out_shape=tuple(jax.ShapeDtypeStruct(a.shape, a.dtype) for a in (skip, lower, weight)),
        in_specs=specs,
        out_specs=specs,
    )(skip, lower, weight)
    return skip[None], lower[None], weight


def solution(mesh):
    in_specs = (
        P("batch", "seq", None),
        P("batch", "seq", "mp"),
        P("batch", "seq", "mp"),
        P(None, None, "mp"),
        P("batch", "seq", None),
        P("batch", "seq"),
        P("batch", "seq", None, "mp"),
    )
    out_specs = (
        P("batch", ("seq", "mp"), None),
        P("batch", ("seq", "mp"), None),
        P(None, "seq", "mp"),
    )
    return jax.shard_map(shards, mesh=mesh, in_specs=in_specs, out_specs=out_specs, check_vma=False)
```

time: 135 us -> 121 us (0.90)
  local copies, waits for them, and re-layouts: 9.05 us -> 1.6 us
  Pallas kernels: 123 us -> 117 us
    pallas_call x1, Pallas kernels: 123 us -> 113 us  [shards(): pl.pallas_call(functools.partial(body, sizes), out_shape=(jax.ShapeDtypeS...]
    unnamed x8 -> x1, local copies, waits for them, and re-layouts: 5.31 us -> 0.83 us
    pallas_call x0 -> x1, Pallas kernels: none -> 4 us  [shards(): pl.pallas_call(hand_over, grid=(steps,), out_shape=tuple((jax.ShapeDtypeS...]
    another operation x1 -> x0, local copies, waits for them, and re-layouts: 2.95 us -> none  [shards(): pair_gradient[0].reshape(endpoints, width)]
where the time goes in v3:
time: 121 us; the launch traced here: 120 us
  Pallas kernels  117 us (97%)
  local copies, waits for them, and re-layouts  1.6 us (1%)
  between operations  1.29 us (1%)
    pallas_call x1, Pallas kernels, shards(): pl.pallas_call(functools.partial(body, sizes), out_shape=(jax.ShapeDtypeS...  113 us
    pallas_call x1, Pallas kernels, shards(): pl.pallas_call(hand_over, grid=(steps,), out_shape=tuple((jax.ShapeDtypeS...  4 us

profile of v3, /device:TPU:1, one launch (start us, length us, event | category | flops | bytes accessed | tf_op | source)
XLA Modules:
  0.0 120.2 jit_solution(11282552725451304532)
XLA Ops:
  1.3 0.8 copy.11
  2.1 0.8 reshape_squeeze.3.rows_ref
  2.9 113.4 %shard_map.94 = (bf16[1024,768]{1,0:T(8,128)(2,1)}, bf16[512,768]{1,0:T(8,128)(2,1)}, f32[5,24,384]{2,1,0:T(8,128)}) custom-call(s32[1,1024]{1,0:T(1,128)} %reshape_squeeze.3.rows_ref, s32[1,1]{1,0:T(1,128)S(6)} %copy.12.count_ref, bf16[512,2,384]{2,1,0:T(2,128)(2,1)} %bitcast.9, bf16[2048,384]{1,0:T(8,128)(2,1)} %bitcast.7, bf16[2048,384]{1,0:T(8,128)(2,1)} %bitcast.8, ...), custom_call_target="tpu_custom_call" | custom-call | tf_op jit(solution)/shard_map/pallas_call | solution.py:709
  116.2 4.0 %shard_map.95 = (bf16[1024,768]{1,0:T(8,128)(2,1)}, bf16[512,768]{1,0:T(8,128)(2,1)}, f32[5,24,384]{2,1,0:T(8,128)}) custom-call(bf16[1024,768]{1,0:T(8,128)(2,1)} %get-tuple-element.9.skip_ref, bf16[512,768]{1,0:T(8,128)(2,1)} %get-tuple-element.10.lower_ref, f32[5,24,384]{2,1,0:T(8,128)} %get-tuple-element.11.weight_ref), custom_call_target="tpu_custom_call" | custom-call | tf_op jit(solution)/shard_map/pallas_call | solution.py:794

commit v4 on v3

--- a/solution.py
+++ b/solution.py
@@ -281,7 +281,7 @@
             lists = jnp.concatenate([four_lists(first + i) for i in range(0, many, 4)], axis=1)
             ends = first + many == n_seq
 
-            @pl.loop(0, tiles)
+            @pl.loop(0, tiles, unroll=4)
             def _(tile, first=first, many=many, lists=lists, ends=ends):
                 wanted = (lists - (tile * TILE).astype(F32)).astype(BF16)
                 wanted = jnp.broadcast_to(wanted, (16, many * cap))
@@ -553,18 +553,17 @@
     for way, part in halves:
         kernel_across(way, part, up).wait_recv()
         kernel_twin(way, part, core).start()
-    junction(1, 1, 2)
     twin_sum(0)
-    junction(1, 2, 5)
+    junction(1, 1, 5)
     slopes_inner(1)
+    slopes_outer(1)
+    weights(1)
+    twin_sum(1)
 
     @pl.loop(0, CHUNKS)
     def _(turn):
         x_sum(0, turn)
 
-    slopes_outer(1)
-    weights(1)
-    twin_sum(1)
     for way, part in halves:
         kernel_twin(way, part, 1 - core).wait_recv()
     loads[4].wait()
@@ -574,6 +573,16 @@
     @pl.loop(0, share_tiles)
     def _(tile):
         input_tile(0, tile)
+
+    @pl.loop(1, n_seq)
+    def _(step):
+        offsets_to(step).wait_send()
+        for part in range(len(LANES)):
+            grads_to(part, step).wait_send()
+
+    for way, part in halves:
+        kernel_across(way, part, up).wait_send()
+        kernel_twin(way, part, core).wait_send()
 
     @pl.loop(0, CHUNKS)
     def _(turn):
@@ -644,15 +653,6 @@
         for copy in outs(tile):
             copy.wait()
 
-    @pl.loop(1, n_seq)
-    def _(step):
-        offsets_to(step).wait_send()
-        for part in range(len(LANES)):
-            grads_to(part, step).wait_send()
-
-    for way, part in halves:
-        kernel_across(way, part, up).wait_send()
-        kernel_twin(way, part, core).wait_send()
     for part in range(len(LANES)):
 
         @pl.when(me > 0)

time: 121 us -> 114 us (0.942)
  Pallas kernels: 117 us -> 111 us
    pallas_call x1, Pallas kernels: 113 us -> 107 us  [shards(): pl.pallas_call(functools.partial(body, sizes), out_shape=(jax.ShapeDtypeS...]
where the time goes in v4:
time: 114 us
  Pallas kernels  111 us (97%)
  local copies, waits for them, and re-layouts  1.6 us (1%)
  between operations  1.45 us (1%)
    pallas_call x1, Pallas kernels, shards(): pl.pallas_call(functools.partial(body, sizes), out_shape=(jax.ShapeDtypeS...  107 us
    pallas_call x1, Pallas kernels, shards(): pl.pallas_call(hand_over, grid=(steps,), out_shape=tuple((jax.ShapeDtypeS...  4 us

profile of v4, /device:TPU:1, one launch (start us, length us, event | category | flops | bytes accessed | tf_op | source)
XLA Modules:
  0.0 114.0 jit_solution(857276613771843190)
XLA Ops:
  1.3 0.8 copy.11
  2.1 0.8 reshape_squeeze.3.rows_ref
  2.9 106.9 %shard_map.94 = (bf16[1024,768]{1,0:T(8,128)(2,1)}, bf16[512,768]{1,0:T(8,128)(2,1)}, f32[5,24,384]{2,1,0:T(8,128)}) custom-call(s32[1,1024]{1,0:T(1,128)} %reshape_squeeze.3.rows_ref, s32[1,1]{1,0:T(1,128)S(6)} %copy.12.count_ref, bf16[512,2,384]{2,1,0:T(2,128)(2,1)} %bitcast.9, bf16[2048,384]{1,0:T(8,128)(2,1)} %bitcast.7, bf16[2048,384]{1,0:T(8,128)(2,1)} %bitcast.8, ...), custom_call_target="tpu_custom_call" | custom-call | tf_op jit(solution)/shard_map/pallas_call | solution.py:709
  109.8 4.0 %shard_map.95 = (bf16[1024,768]{1,0:T(8,128)(2,1)}, bf16[512,768]{1,0:T(8,128)(2,1)}, f32[5,24,384]{2,1,0:T(8,128)}) custom-call(bf16[1024,768]{1,0:T(8,128)(2,1)} %get-tuple-element.9.skip_ref, bf16[512,768]{1,0:T(8,128)(2,1)} %get-tuple-element.10.lower_ref, f32[5,24,384]{2,1,0:T(8,128)} %get-tuple-element.11.weight_ref), custom_call_target="tpu_custom_call" | custom-call | tf_op jit(solution)/shard_map/pallas_call | solution.py:794

commit v5 on v4

--- a/solution.py
+++ b/solution.py
@@ -281,7 +281,7 @@
             lists = jnp.concatenate([four_lists(first + i) for i in range(0, many, 4)], axis=1)
             ends = first + many == n_seq
 
-            @pl.loop(0, tiles, unroll=4)
+            @pl.loop(0, tiles, unroll=8)
             def _(tile, first=first, many=many, lists=lists, ends=ends):
                 wanted = (lists - (tile * TILE).astype(F32)).astype(BF16)
                 wanted = jnp.broadcast_to(wanted, (16, many * cap))

time: 114 us -> 114 us (level)
  no operation moved by 1% of the time
where the time goes in v5:
time: 114 us; the launch traced here: 113 us
  Pallas kernels  110 us (96%)
  local copies, waits for them, and re-layouts  1.6 us (1%)
  between operations  1.45 us (1%)
    pallas_call x1, Pallas kernels, shards(): pl.pallas_call(functools.partial(body, sizes), out_shape=(jax.ShapeDtypeS...  106 us
    pallas_call x1, Pallas kernels, shards(): pl.pallas_call(hand_over, grid=(steps,), out_shape=tuple((jax.ShapeDtypeS...  4 us

profile of v5, /device:TPU:1, one launch (start us, length us, event | category | flops | bytes accessed | tf_op | source)
XLA Modules:
  0.0 113.3 jit_solution(5120785188642409370)
XLA Ops:
  1.3 0.8 copy.11
  2.1 0.8 reshape_squeeze.3.rows_ref
  2.9 106.3 %shard_map.94 = (bf16[1024,768]{1,0:T(8,128)(2,1)}, bf16[512,768]{1,0:T(8,128)(2,1)}, f32[5,24,384]{2,1,0:T(8,128)}) custom-call(s32[1,1024]{1,0:T(1,128)} %reshape_squeeze.3.rows_ref, s32[1,1]{1,0:T(1,128)S(6)} %copy.12.count_ref, bf16[512,2,384]{2,1,0:T(2,128)(2,1)} %bitcast.9, bf16[2048,384]{1,0:T(8,128)(2,1)} %bitcast.7, bf16[2048,384]{1,0:T(8,128)(2,1)} %bitcast.8, ...), custom_call_target="tpu_custom_call" | custom-call | tf_op jit(solution)/shard_map/pallas_call | solution.py:709
  109.2 4.0 %shard_map.95 = (bf16[1024,768]{1,0:T(8,128)(2,1)}, bf16[512,768]{1,0:T(8,128)(2,1)}, f32[5,24,384]{2,1,0:T(8,128)}) custom-call(bf16[1024,768]{1,0:T(8,128)(2,1)} %get-tuple-element.9.skip_ref, bf16[512,768]{1,0:T(8,128)(2,1)} %get-tuple-element.10.lower_ref, f32[5,24,384]{2,1,0:T(8,128)} %get-tuple-element.11.weight_ref), custom_call_target="tpu_custom_call" | custom-call | tf_op jit(solution)/shard_map/pallas_call | solution.py:794
